TPU v7x, 32 devices: a whole 2x2x4 slice. The times are simulated.
32 devices in a mesh: outer: 8 (over z, core), inner: 4 (over y, x).
Axes of the slice: x: 2, y: 2, z: 4, core: 2. Of those that a mesh axis runs over, the one named last changes fastest.
Arguments:
- queries: bfloat16 [4096, 32, 128], P(('outer', 'inner')), may hold values from -8 to 8
- keys: bfloat16 [4096, 4, 128], P(('outer', 'inner')), may hold values from -8 to 8
- values: bfloat16 [4096, 4, 128], P(('outer', 'inner')), may hold values from -6 to 6
- positions: int32 [4096], P(('outer', 'inner')), may hold values from 0 to 4095, as said below
Outputs:
- attended: bfloat16 [4096, 32, 128], P(('outer', 'inner'))
Inputs may be any that keep to these rules, and one draw needn't show every extreme that they name: positions is a permutation of the numbers 0 to 4095 made of runs of 64 consecutive ascending positions starting at multiples of 64; runs are laid out in an order drawn from the seed.
All inputs are finite; a program needn't handle non-finite values.
Results may differ from a plain program's by a relative error of at most 0.0045.
Values may be sent and summed in bfloat16 or wider, within the bound.
No kernel may reach another device: no remote copies, remote signals or barrier semaphores. Data moves between devices by JAX's collectives and lax.ppermute only.
A program may use at most 128 MiB of HBM per device.

v0:
```python
import functools
import math

import jax
import jax.numpy as jnp
from jax import lax
from jax.experimental import pallas as pl
from jax.experimental.pallas import tpu as pltpu
from jax.sharding import PartitionSpec as P

RUN = 64
TILE = 8
KEEP = 4
AXES = ("outer", "inner")


def flash(score, v, state, factor, live=None):
    top, total, mixed = state
    keys = score.shape[1]
    if isinstance(live, int):
        lane = lax.broadcasted_iota(jnp.int32, score.shape, 1)
        keys, live = live, lane < live
    if live is not None:
        score = jnp.where(live, score, -jnp.inf)
    parts = [score[:, c : c + 128] for c in range(0, score.shape[1], 128)]
    new = jnp.max(functools.reduce(jnp.maximum, parts), axis=1, keepdims=True)
    if top is None:
        new = jnp.broadcast_to(new, parts[0].shape)
    else:
        new = jnp.maximum(top, new)
    weights = [jnp.exp2((part - new) * factor) for part in parts]
    part_total = functools.reduce(jnp.add, weights)
    weights = jnp.concatenate([w.astype(jnp.bfloat16) for w in weights], axis=1)
    part_mixed = jnp.dot(weights[:, :keys], v, preferred_element_type=jnp.float32)
    if top is None:
        return new, part_total, part_mixed
    decay = jnp.exp2((top - new) * factor)
    return new, total * decay + part_total, mixed * decay + part_mixed


def head_tile(q_ref, state_refs, a, keys, values, factor, live=None):
    def scores(h):
        return lax.dot_general(
            q_ref[a, h],
            keys(h),
            (((1,), (1,)), ((), ())),
            preferred_element_type=jnp.float32,
        )

    heads_kv = q_ref.shape[1]
    ahead = scores(0)
    for h in range(heads_kv):
        score = ahead
        if h + 1 < heads_kv:
            ahead = scores(h + 1)
        state = (None, None, None)
        if live is None or isinstance(live, int):
            state = tuple(ref[a, h] for ref in state_refs)
        state = flash(score, values(h), state, factor, live)
        for ref, value in zip(state_refs, state):
            ref[a, h] = value


def own_kernel(group, factor, half, q_ref, own_ref, meta_ref, *refs):
    heads_kv, rows, head_dim = q_ref.shape[1:]
    state_refs = refs[:3]
    run_rows = 2 * heads_kv * RUN

    ids = own_ref[2 * run_rows :].astype(jnp.float32)
    lane = lax.broadcasted_iota(jnp.int32, ids.shape, 1)
    numbers = [jnp.max(jnp.where(lane // RUN == a, ids, 0.0)) for a in range(2)]
    row = lax.broadcasted_iota(jnp.int32, meta_ref.shape, 0)
    meta_ref[...] = jnp.where(
        row == 0, numbers[0], jnp.where(row == 1, numbers[1], 0.0)
    )

    row_at = lax.broadcasted_iota(jnp.int32, (rows, 2 * RUN), 0) // group
    key_at = lax.broadcasted_iota(jnp.int32, (rows, 2 * RUN), 1)
    for a in range(2):
        mine, other = numbers[a], numbers[1 - a]
        seen = (other < mine) & ((other >= half) == (mine >= half))
        reach = jnp.where(seen, RUN, 0)
        if a == 0:
            live = (key_at <= row_at) | ((key_at >= RUN) & (key_at < RUN + reach))
        else:
            live = (key_at < reach) | ((key_at >= RUN) & (key_at - RUN <= row_at))

        def own(g):
            starts = [g * RUN, run_rows + g * RUN]
            return jnp.concatenate([own_ref[n : n + RUN] for n in starts])

        head_tile(q_ref, state_refs, a, own, lambda h: own(heads_kv + h), factor, live)


def attend_kernel(group, factor, half, last, blocks, q_ref, *refs):
    heads_kv, rows, head_dim = q_ref.shape[1:]
    run_rows = 2 * heads_kv * RUN
    block_rows = 2 * run_rows + 16
    kv_refs, refs = refs[: len(blocks)], refs[len(blocks) :]
    refs = refs[5:]
    if last:
        out_ref, refs = refs[0], refs[1:]
    meta_ref, *state_refs, buf = refs

    meta = meta_ref[...]
    counts = tuple(
        jnp.max(meta[2 + a : 3 + a]).astype(jnp.int32) for a in range(2)
    )
    seen_bits = []
    for ref, (skip, end) in zip(kv_refs, blocks):
        assert end - skip <= 8
        ids = jnp.concatenate(
            [ref[n * block_rows - 16 : n * block_rows] for n in range(skip + 1, end + 1)]
        ).astype(jnp.float32)
        row = lax.broadcasted_iota(jnp.int32, ids.shape, 0)
        lane = lax.broadcasted_iota(jnp.int32, ids.shape, 1)
        bit = jnp.left_shift(1, 2 * (row // 16) + lane // RUN)
        bit = jnp.where((row % 16 == 0) & (lane % RUN == 0), bit, 0).astype(jnp.float32)
        found = []
        for a in range(2):
            mine = meta[a : a + 1]
            low = jnp.where(mine >= half, float(half), 0.0)
            seen = (ids < mine) & (ids >= low)
            found.append(jnp.sum(jnp.where(seen, bit, 0.0)).astype(jnp.int32))
        seen_bits.append(found)

    for ref, (skip, end), bits in zip(kv_refs, blocks, seen_bits):

        def gather(n, counts):
            at = pl.multiple_of((skip + n // 2) * block_rows + n % 2 * run_rows, 16)
            fresh = []
            for a in range(2):
                flag = (bits[a] >> n) & 1
                count = counts[a]

                @pl.when(flag == 1)
                def _():
                    buf[a, count] = ref[pl.ds(at, run_rows), :]

                fresh.append(count + flag)
            return tuple(fresh)

        counts = lax.fori_loop(0, 2 * (end - skip), gather, counts)

    def some_runs(a, start, runs):
        def rows_of(g):
            found = buf[a, pl.ds(start, runs), g * RUN : (g + 1) * RUN, :]
            return found.reshape(runs * RUN, -1)

        def keys(h):
            if runs > 1:
                return rows_of(h)
            return jnp.concatenate([rows_of(h), jnp.zeros((RUN, head_dim), buf.dtype)])

        live = RUN if runs == 1 else None
        head_tile(
            q_ref, state_refs, a, keys, lambda h: rows_of(heads_kv + h), factor, live
        )

    whole = [count // TILE for count in counts]

    def step(item, carry):
        a = (item >= whole[0]).astype(jnp.int32)
        some_runs(a, (item - a * whole[0]) * TILE, TILE)
        return carry

    lax.fori_loop(0, whole[0] + whole[1], step, 0)

    def remainder(a, carry):
        count = jnp.where(a == 0, counts[0], counts[1])
        start = count // TILE * TILE
        runs = TILE // 2
        while runs >= (1 if last else KEEP):

            @pl.when(count & runs != 0)
            def _():
                some_runs(a, start, runs)

            start = start + (count & runs)
            runs //= 2
        return carry

    lax.fori_loop(0, 2, remainder, 0)

    if not last:
        row = lax.broadcasted_iota(jnp.int32, meta.shape, 0)
        for a in range(2):
            start = counts[a] // KEEP * KEEP
            rest = counts[a] - start

            @pl.when((start > 0) & (rest > 0))
            def _():
                for n in range(KEEP - 1):
                    buf[a, n] = buf[a, start + n]

            meta = jnp.where(row == 2 + a, rest.astype(jnp.float32), meta)
        meta_ref[...] = meta
        return

    for a in range(2):
        for h in range(0, heads_kv, 2):
            done = []
            for g in (h, h + 1):
                total = jnp.sum(state_refs[1][a, g], axis=1, keepdims=True)
                part = state_refs[2][a, g] * (1.0 / total)
                done.append(part.reshape(RUN, group, -1))
            out_ref[a * RUN : (a + 1) * RUN, h * group : (h + 2) * group, :] = (
                jnp.concatenate(done, axis=1).astype(out_ref.dtype)
            )


class Attention:
    def __init__(self, q, group, half, room):
        self.q, self.group, self.half = q, group, half
        self.factor = math.log2(math.e) / math.sqrt(q.shape[3])
        heads_kv, rows, head_dim = q.shape[1:]
        self.block_rows = 4 * heads_kv * RUN + 16
        slots = 2 * room + KEEP
        self.carried = [jax.ShapeDtypeStruct((8, 128), jnp.float32)]
        self.carried += [
            jax.ShapeDtypeStruct((2, heads_kv, rows, n), jnp.float32)
            for n in (128, 128, head_dim)
        ]
        self.carried.append(
            jax.ShapeDtypeStruct((2, slots, 2 * heads_kv * RUN, head_dim), q.dtype)
        )

    def call(self, kernel, operands, shapes, aliases, count, name):
        vmem = pl.BlockSpec(memory_space=pltpu.VMEM)
        return pl.pallas_call(
            kernel,
            out_shape=shapes,
            in_specs=[vmem] * len(operands),
            out_specs=[vmem] * len(shapes),
            input_output_aliases=aliases,
            compiler_params=pltpu.CompilerParams(vmem_limit_bytes=28 * 1024 * 1024),
            cost_estimate=pl.CostEstimate(
                flops=count * RUN * self.q.size * 4,
                bytes_accessed=self.q.size * 8,
                transcendentals=0,
            ),
            name=name,
        )(*operands)

    def start(self, own):
        kernel = functools.partial(own_kernel, self.group, self.factor, self.half)
        return self.call(kernel, [self.q, own], self.carried, {}, 2, "attend_own")

    def add(self, state, kvs, out=None):
        kvs = [x if isinstance(x, tuple) else (x, 0) for x in kvs]
        blocks = [(skip, x.shape[0] // self.block_rows) for x, skip in kvs]
        count = sum(end - skip for skip, end in blocks)
        operands = [self.q, *(x for x, _ in kvs), *state]
        first, ahead = 1 + len(kvs), int(out is not None)
        aliases = {first + n: ahead + n for n in range(len(state))}
        shapes = ([out] if ahead else []) + self.carried
        kernel = functools.partial(
            attend_kernel, self.group, self.factor, self.half, out is not None, blocks
        )
        results = self.call(kernel, operands, shapes, aliases, count, "attend")
        return results[0] if ahead else results


def per_device(queries, keys, values, positions):
    outer, inner = lax.axis_size("outer"), lax.axis_size("inner")
    tokens, heads_q, head_dim = queries.shape
    heads_kv = keys.shape[1]
    group = heads_q // heads_kv
    half = tokens // RUN * outer * inner // 2

    chips = outer // 2
    bits = inner.bit_length() - 1
    ring = [0] + list(range(1, chips, 2)) + list(range(2, chips, 2))[::-1]
    after = {ring[n]: ring[(n + 1) % chips] for n in range(chips)}

    def permute(x, to):
        pairs = []
        for z in range(chips):
            for core in range(2):
                for place in range(inner):
                    nz, ncore, nplace = to(z, core, place)
                    pairs.append(
                        (
                            (2 * z + core) * inner + place,
                            (2 * nz + ncore) * inner + nplace,
                        )
                    )
        return lax.ppermute(x, AXES, pairs)

    def along_z(x):
        return permute(x, lambda z, core, place: (after[z], core, place))

    def over_place(x, step):
        def to(z, core, place):
            return z, core, place ^ (1 << (bits - 1 - step if core else step))

        return permute(x, to)

    def other_core(x):
        return permute(x, lambda z, core, place: (z, 1 - core, place))

    def tied(x, *others):
        return lax.optimization_barrier((x, *others))[0]

    by_run = jnp.concatenate(
        [x.reshape(2, RUN, heads_kv, head_dim) for x in (keys, values)], axis=2
    ).transpose(0, 2, 1, 3)
    numbers = (positions // RUN).astype(jnp.bfloat16)
    own = jnp.concatenate(
        [
            by_run.reshape(-1, head_dim),
            jnp.broadcast_to(numbers[None, :], (16, head_dim)),
        ]
    )
    q = (
        queries.reshape(2, RUN, heads_kv, group, head_dim)
        .transpose(0, 2, 1, 3, 4)
        .reshape(2, heads_kv, RUN * group, head_dim)
    )

    attention = Attention(q, group, half, 2 * inner)
    state = attention.start(own)

    stage, waiting = own, None
    for n in range(chips - 1):
        following = along_z(stage)
        held = stage
        for step in range(bits):
            if n == 0 and step == 1:
                held = tied(held, following, state[0])
            held = jnp.concatenate([held, over_place(held, step)])
        if waiting:
            state = attention.add(state, waiting)
            held = tied(held, state[0])
        waiting = [(held, int(n == 0)), other_core(held)]
        stage = following

    found = [stage]
    for step in range(bits):
        found += [over_place(x, step) for x in found]
    *most, final = found
    most = jnp.concatenate(most)
    theirs = other_core(most)
    state = attention.add(state, waiting)
    state = attention.add(state, [most, theirs])
    final = tied(final, state[0])
    theirs = other_core(final)
    state = attention.add(state, [final])
    out = jax.ShapeDtypeStruct(queries.shape, queries.dtype)
    return attention.add(state, [theirs], out)


def solution(mesh):
    in_specs = (
        P(("outer", "inner"), None, None),
        P(("outer", "inner"), None, None),
        P(("outer", "inner"), None, None),
        P(("outer", "inner")),
    )
    out_specs = P(("outer", "inner"), None, None)
    return jax.shard_map(
        per_device, mesh=mesh, in_specs=in_specs, out_specs=out_specs, check_vma=False
    )
```

profile of v0, /device:TPU:1, one launch (start us, length us, event | category | flops | bytes accessed | tf_op | source)
XLA Modules:
  0.0 64.6 jit_solution(4857511709855522408)
XLA Ops:
  0.0 1.0 %copy.36 = bf16[2,64,4,128]{3,1,2,0:T(8,128)(2,1)S(1)} copy(bf16[2,64,4,128]{3,2,1,0:T(4,128)(2,1)} %bitcast.21) | data formatting | bytes 262144 | tf_op jit(solution)/shard_map/reshape | solution.py:306
  1.0 0.9 %copy.37 = bf16[2,64,4,128]{3,1,2,0:T(8,128)(2,1)S(1)} copy(bf16[2,64,4,128]{3,2,1,0:T(4,128)(2,1)} %bitcast.22) | data formatting | bytes 262144 | tf_op jit(solution)/shard_map/reshape | solution.py:306
  1.9 0.7 %fusion = bf16[128]{0:T(256)(128)(2,1)S(1)} fusion(s32[128]{0:T(128)} %param.7), kind=kLoop, calls=%fused_computation.17 | loop fusion | flops 2048 | bytes 768 | tf_op jit(solution)/shard_map/convert_element_type | solution.py:308
  2.7 2.1 %collective-permute-start.11 = (bf16[1040,128]{1,0:T(8,128)(2,1)S(1)}, bf16[1040,128]{1,0:T(8,128)(2,1)S(1)}, u32[]{:S(2)}, u32[]{:S(2)}) collective-permute-start(bf16[1040,128]{1,0:T(8,128)(2,1)S(1)} %pad_maximum_fusion.5.own_ref), channel_id=1, source_target_pairs={{0,1},{1,0},{2,3},{3,2},{4,6},{5,7},{6,4},{7,5},{8,9},{9,8},{10,11... | collective-permute-start | bytes 798728 | tf_op jit(solution)/shard_map/ppermute | solution.py:288
  4.8 1.3 %collective-permute-start = (bf16[1040,128]{1,0:T(8,128)(2,1)S(1)}, bf16[1040,128]{1,0:T(8,128)(2,1)S(1)}, u32[]{:S(2)}, u32[]{:S(2)}) collective-permute-start(bf16[1040,128]{1,0:T(8,128)(2,1)S(1)} %pad_maximum_fusion.5.own_ref), channel_id=1, source_target_pairs={{0,8},{1,9},{2,10},{3,11},{4,12},{5,13},{6,14},{7,15},{8,24},{9,25... | collective-permute-start | bytes 798728 | tf_op jit(solution)/shard_map/ppermute | solution.py:288
  6.1 0.2 copy.39
  6.3 1.2 %attend_own.1 = (f32[8,128]{1,0:T(8,128)S(1)}, f32[2,4,512,128]{3,2,1,0:T(8,128)S(1)}, f32[2,4,512,128]{3,2,1,0:T(8,128)S(1)}, f32[2,4,512,128]{3,2,1,0:T(8,128)S(1)}, bf16[2,20,512,128]{3,2,1,0:T(8,128)(2,1)S(1)}) custom-call(bf16[2,4,512,128]{3,2,1,0:T(8,128)(2,1)S(1)} %bitcast.11, bf16[1040,128]{1,0:T(8,128)(2,1)S(1)} %pad_maximum_fusion.5.own_ref), custom_call_target="tpu_custom_call" | custom-call | flops 268435456 | bytes 4194304 | tf_op jit(solution)/shard_map/attend_own/pallas_call | solution.py:230
  7.5 1.4 %collective-permute-done.11 = bf16[1040,128]{1,0:T(8,128)(2,1)S(1)} collective-permute-done((bf16[1040,128]{1,0:T(8,128)(2,1)S(1)}, bf16[1040,128]{1,0:T(8,128)(2,1)S(1)}, u32[]{:S(2)}, u32[]{:S(2)}) %collective-permute-start.11) | collective-permute-done | bytes 266272 | tf_op jit(solution)/shard_map/ppermute | solution.py:288
  9.0 3.7 %collective-permute-done = bf16[1040,128]{1,0:T(8,128)(2,1)S(1)} collective-permute-done((bf16[1040,128]{1,0:T(8,128)(2,1)S(1)}, bf16[1040,128]{1,0:T(8,128)(2,1)S(1)}, u32[]{:S(2)}, u32[]{:S(2)}) %collective-permute-start) | collective-permute-done | bytes 266272 | tf_op jit(solution)/shard_map/ppermute | solution.py:288
  12.7 2.5 %collective-permute-start.12 = (bf16[2080,128]{1,0:T(8,128)(2,1)S(1)}, bf16[2080,128]{1,0:T(8,128)(2,1)S(1)}, u32[]{:S(2)}, u32[]{:S(2)}) collective-permute-start(bf16[2080,128]{1,0:T(8,128)(2,1)S(1)} %pad_maximum_fusion.4), channel_id=1, source_target_pairs={{0,2},{1,3},{2,0},{3,1},{4,5},{5,4},{6,7},{7,6},{8,10},{9,11},{10,... | collective-permute-start | bytes 1597448 | tf_op jit(solution)/shard_map/ppermute | solution.py:288
  15.2 0.0 collective-permute-start.9
  15.3 0.3 collective-permute-start.1
  15.6 8.1 %collective-permute-done.9 = bf16[1040,128]{1,0:T(8,128)(2,1)S(1)} collective-permute-done((bf16[1040,128]{1,0:T(8,128)(2,1)S(1)}, bf16[1040,128]{1,0:T(8,128)(2,1)S(1)}, u32[]{:S(2)}, u32[]{:S(2)}) %collective-permute-start.9) | collective-permute-done | bytes 266272 | tf_op jit(solution)/shard_map/ppermute | solution.py:288
  23.7 0.1 collective-permute-start.10
  23.8 0.0 collective-permute-done.1
  23.8 0.7 %collective-permute-start.7 = (bf16[1040,128]{1,0:T(8,128)(2,1)S(1)}, bf16[1040,128]{1,0:T(8,128)(2,1)S(1)}, u32[]{:S(2)}, u32[]{:S(2)}) collective-permute-start(bf16[1040,128]{1,0:T(8,128)(2,1)S(1)} %collective-permute-done.1), channel_id=1, source_target_pairs={{0,1},{1,0},{2,3},{3,2},{4,6},{5,7},{6,4},{7,5},{8,9},{9,8},{10,11... | collective-permute-start | bytes 798728 | tf_op jit(solution)/shard_map/ppermute | solution.py:288
  24.5 0.5 collective-permute-done.12
  25.0 0.1 constant_dynamic-update-slice_fusion.3.refs_0_
  25.1 1.7 %collective-permute-start.13 = (bf16[4160,128]{1,0:T(8,128)(2,1)S(1)}, bf16[4160,128]{1,0:T(8,128)(2,1)S(1)}, u32[]{:S(2)}, u32[]{:S(2)}) collective-permute-start(bf16[4160,128]{1,0:T(8,128)(2,1)S(1)} %constant_dynamic-update-slice_fusion.3.refs_0_), channel_id=1, source_target_pairs={{0,4},{1,5},{2,6},{3,7},{4,0},{5,1},{6,2},{7,3},{8,12},{9,13},{10,... | collective-permute-start | bytes 3194888 | tf_op jit(solution)/shard_map/ppermute | solution.py:288
  26.8 0.5 collective-permute-start.2
  27.3 3.9 %collective-permute-done.7 = bf16[1040,128]{1,0:T(8,128)(2,1)S(1)} collective-permute-done((bf16[1040,128]{1,0:T(8,128)(2,1)S(1)}, bf16[1040,128]{1,0:T(8,128)(2,1)S(1)}, u32[]{:S(2)}, u32[]{:S(2)}) %collective-permute-start.7) | collective-permute-done | bytes 266272 | tf_op jit(solution)/shard_map/ppermute | solution.py:288
  31.3 1.6 %collective-permute-start.8 = (bf16[2080,128]{1,0:T(8,128)(2,1)S(1)}, bf16[2080,128]{1,0:T(8,128)(2,1)S(1)}, u32[]{:S(2)}, u32[]{:S(2)}) collective-permute-start(bf16[2080,128]{1,0:T(8,128)(2,1)S(1)} %pad_maximum_fusion.2), channel_id=1, source_target_pairs={{0,2},{1,3},{2,0},{3,1},{4,5},{5,4},{6,7},{7,6},{8,10},{9,11},{10,... | collective-permute-start | bytes 1597448 | tf_op jit(solution)/shard_map/ppermute | solution.py:288
  32.9 2.2 %collective-permute-done.10 = bf16[2080,128]{1,0:T(8,128)(2,1)S(1)} collective-permute-done((bf16[2080,128]{1,0:T(8,128)(2,1)S(1)}, bf16[2080,128]{1,0:T(8,128)(2,1)S(1)}, u32[]{:S(2)}, u32[]{:S(2)}) %collective-permute-start.10) | collective-permute-done | bytes 532512 | tf_op jit(solution)/shard_map/ppermute | solution.py:288
  35.0 0.1 pad_maximum_fusion.1.refs_0_
  35.1 0.0 collective-permute-done.13.refs_1_
  35.1 2.3 %attend.6 = (f32[8,128]{1,0:T(8,128)S(1)}, f32[2,4,512,128]{3,2,1,0:T(8,128)S(1)}, f32[2,4,512,128]{3,2,1,0:T(8,128)S(1)}, f32[2,4,512,128]{3,2,1,0:T(8,128)S(1)}, bf16[2,20,512,128]{3,2,1,0:T(8,128)(2,1)S(1)}) custom-call(bf16[2,4,512,128]{3,2,1,0:T(8,128)(2,1)S(1)} %bitcast.12, ...), custom_call_target="tpu_custom_call", output_to_operand_aliasing={{0}: (3, {}), {1}: (4, {}), {2}: (5, {}), {3}: (6, {}), {4}... | custom-call | flops 939524096 | bytes 4194304 | tf_op jit(solution)/shard_map/attend/pallas_call | solution.py:230
  37.4 0.2 collective-permute-start.14
  37.6 0.0 collective-permute-done.2
  37.6 0.4 collective-permute-start.3
  38.0 1.1 %collective-permute-start.5 = (bf16[1040,128]{1,0:T(8,128)(2,1)S(1)}, bf16[1040,128]{1,0:T(8,128)(2,1)S(1)}, u32[]{:S(2)}, u32[]{:S(2)}) collective-permute-start(bf16[1040,128]{1,0:T(8,128)(2,1)S(1)} %collective-permute-done.2), channel_id=1, source_target_pairs={{0,2},{1,3},{2,0},{3,1},{4,5},{5,4},{6,7},{7,6},{8,10},{9,11},{10,... | collective-permute-start | bytes 798728 | tf_op jit(solution)/shard_map/ppermute | solution.py:288
  39.1 1.6 %collective-permute-done.8 = bf16[2080,128]{1,0:T(8,128)(2,1)S(1)} collective-permute-done((bf16[2080,128]{1,0:T(8,128)(2,1)S(1)}, bf16[2080,128]{1,0:T(8,128)(2,1)S(1)}, u32[]{:S(2)}, u32[]{:S(2)}) %collective-permute-start.8) | collective-permute-done | bytes 532512 | tf_op jit(solution)/shard_map/ppermute | solution.py:288
  40.7 0.1 pad_maximum_fusion.refs_0_
  40.8 0.0 collective-permute-done.14.refs_1_
  40.8 3.6 %attend.7 = (f32[8,128]{1,0:T(8,128)S(1)}, f32[2,4,512,128]{3,2,1,0:T(8,128)S(1)}, f32[2,4,512,128]{3,2,1,0:T(8,128)S(1)}, f32[2,4,512,128]{3,2,1,0:T(8,128)S(1)}, bf16[2,20,512,128]{3,2,1,0:T(8,128)(2,1)S(1)}) custom-call(bf16[2,4,512,128]{3,2,1,0:T(8,128)(2,1)S(1)} %bitcast.13, ...), custom_call_target="tpu_custom_call", output_to_operand_aliasing={{0}: (3, {}), {1}: (4, {}), {2}: (5, {}), {3}: (6, {}), {4}... | custom-call | flops 1073741824 | bytes 4194304 | tf_op jit(solution)/shard_map/attend/pallas_call | solution.py:230
  44.4 4.1 %collective-permute-start.15 = (bf16[4160,128]{1,0:T(8,128)(2,1)S(1)}, bf16[4160,128]{1,0:T(8,128)(2,1)S(1)}, u32[]{:S(2)}, u32[]{:S(2)}) collective-permute-start(bf16[4160,128]{1,0:T(8,128)(2,1)S(1)} %pad_maximum_fusion.refs_0_), channel_id=1, source_target_pairs={{0,4},{1,5},{2,6},{3,7},{4,0},{5,1},{6,2},{7,3},{8,12},{9,13},{10,... | collective-permute-start | bytes 3194888 | tf_op jit(solution)/shard_map/ppermute | solution.py:288
  48.5 0.0 collective-permute-done.3
  48.6 0.0 collective-permute-done.5
  48.6 0.9 %collective-permute-start.6 = (bf16[3120,128]{1,0:T(8,128)(2,1)S(1)}, bf16[3120,128]{1,0:T(8,128)(2,1)S(1)}, u32[]{:S(2)}, u32[]{:S(2)}) collective-permute-start(bf16[3120,128]{1,0:T(8,128)(2,1)S(1)} %constant_dynamic-update-slice_fusion.refs_0_), channel_id=1, source_target_pairs={{0,4},{1,5},{2,6},{3,7},{4,0},{5,1},{6,2},{7,3},{8,12},{9,13},{10,... | collective-permute-start | bytes 2396168 | tf_op jit(solution)/shard_map/ppermute | solution.py:288
  49.6 1.5 %collective-permute-start.4 = (bf16[1040,128]{1,0:T(8,128)(2,1)S(1)}, bf16[1040,128]{1,0:T(8,128)(2,1)S(1)}, u32[]{:S(2)}, u32[]{:S(2)}) collective-permute-start(bf16[1040,128]{1,0:T(8,128)(2,1)S(1)} %collective-permute-done.3), channel_id=1, source_target_pairs={{0,2},{1,3},{2,0},{3,1},{4,5},{5,4},{6,7},{7,6},{8,10},{9,11},{10,... | collective-permute-start | bytes 798728 | tf_op jit(solution)/shard_map/ppermute | solution.py:288
  51.0 0.0 collective-permute-done.15.refs_1_
  51.0 4.1 %attend.8 = (f32[8,128]{1,0:T(8,128)S(1)}, f32[2,4,512,128]{3,2,1,0:T(8,128)S(1)}, f32[2,4,512,128]{3,2,1,0:T(8,128)S(1)}, f32[2,4,512,128]{3,2,1,0:T(8,128)S(1)}, bf16[2,20,512,128]{3,2,1,0:T(8,128)(2,1)S(1)}) custom-call(bf16[2,4,512,128]{3,2,1,0:T(8,128)(2,1)S(1)} %bitcast.14, ...), custom_call_target="tpu_custom_call", output_to_operand_aliasing={{0}: (3, {}), {1}: (4, {}), {2}: (5, {}), {3}: (6, {}), {4}... | custom-call | flops 1073741824 | bytes 4194304 | tf_op jit(solution)/shard_map/attend/pallas_call | solution.py:230
  55.2 0.0 collective-permute-done.6.refs_1_
  55.2 3.6 %attend.9 = (f32[8,128]{1,0:T(8,128)S(1)}, f32[2,4,512,128]{3,2,1,0:T(8,128)S(1)}, f32[2,4,512,128]{3,2,1,0:T(8,128)S(1)}, f32[2,4,512,128]{3,2,1,0:T(8,128)S(1)}, bf16[2,20,512,128]{3,2,1,0:T(8,128)(2,1)S(1)}) custom-call(bf16[2,4,512,128]{3,2,1,0:T(8,128)(2,1)S(1)} %bitcast.15, ...), custom_call_target="tpu_custom_call", output_to_operand_aliasing={{0}: (3, {}), {1}: (4, {}), {2}: (5, {}), {3}: (6, {}), {4}... | custom-call | flops 805306368 | bytes 4194304 | tf_op jit(solution)/shard_map/attend/pallas_call | solution.py:230
  58.8 0.0 collective-permute-done.4.refs_0_
  58.8 0.1 collective-permute-start.16
  58.9 0.3 attend.10
  59.2 1.3 %collective-permute-done.16.refs_0_ = bf16[1040,128]{1,0:T(8,128)(2,1)S(1)} collective-permute-done((bf16[1040,128]{1,0:T(8,128)(2,1)S(1)}, bf16[1040,128]{1,0:T(8,128)(2,1)S(1)}, u32[]{:S(2)}, u32[]{:S(2)}) %collective-permute-start.16) | collective-permute-done | bytes 266272 | tf_op jit(solution)/shard_map/ppermute | solution.py:288
  60.4 4.2 %attend.11 = (bf16[128,32,128]{2,1,0:T(8,128)(2,1)}, f32[8,128]{1,0:T(8,128)S(1)}, f32[2,4,512,128]{3,2,1,0:T(8,128)S(1)}, f32[2,4,512,128]{3,2,1,0:T(8,128)S(1)...) custom-call(bf16[2,4,512,128]{3,2,1,0:T(8,128)(2,1)S(1)} %bitcast.17, ...), custom_call_target="tpu_custom_call", output_to_operand_aliasing={{1}: (2, {}), {2}: (3, {}), {3}: (4, {}), {4}: (5, {}), {5}... | custom-call | flops 134217728 | bytes 4194304 | tf_op jit(solution)/shard_map/attend/pallas_call | solution.py:230
  (12 shorter events, 0.3 us)
Async XLA Ops:
  0.0 6.1 %copy-start = (bf16[128,32,128]{2,1,0:T(8,128)(2,1)S(1)}, bf16[128,32,128]{2,1,0:T(8,128)(2,1)}, u32[]{:S(2)}) copy-start(bf16[128,32,128]{2,1,0:T(8,128)(2,1)} %param.4) | copy-start | bytes 3145732
  2.7 6.2 %collective-permute-start.11 = (bf16[1040,128]{1,0:T(8,128)(2,1)S(1)}, bf16[1040,128]{1,0:T(8,128)(2,1)S(1)}, u32[]{:S(2)}, u32[]{:S(2)}) collective-permute-start(bf16[1040,128]{1,0:T(8,128)(2,1)S(1)} %pad_maximum_fusion.5.own_ref), channel_id=1, source_target_pairs={{0,1},{1,0},{2,3},{3,2},{4,6},{5,7},{6,4},{7,5},{8,9},{9,8},{10,11... | collective-permute-start | bytes 798728 | tf_op jit(solution)/shard_map/ppermute | solution.py:288
  4.8 7.9 %collective-permute-start = (bf16[1040,128]{1,0:T(8,128)(2,1)S(1)}, bf16[1040,128]{1,0:T(8,128)(2,1)S(1)}, u32[]{:S(2)}, u32[]{:S(2)}) collective-permute-start(bf16[1040,128]{1,0:T(8,128)(2,1)S(1)} %pad_maximum_fusion.5.own_ref), channel_id=1, source_target_pairs={{0,8},{1,9},{2,10},{3,11},{4,12},{5,13},{6,14},{7,15},{8,24},{9,25... | collective-permute-start | bytes 798728 | tf_op jit(solution)/shard_map/ppermute | solution.py:288
  12.7 12.4 %collective-permute-start.12 = (bf16[2080,128]{1,0:T(8,128)(2,1)S(1)}, bf16[2080,128]{1,0:T(8,128)(2,1)S(1)}, u32[]{:S(2)}, u32[]{:S(2)}) collective-permute-start(bf16[2080,128]{1,0:T(8,128)(2,1)S(1)} %pad_maximum_fusion.4), channel_id=1, source_target_pairs={{0,2},{1,3},{2,0},{3,1},{4,5},{5,4},{6,7},{7,6},{8,10},{9,11},{10,... | collective-permute-start | bytes 1597448 | tf_op jit(solution)/shard_map/ppermute | solution.py:288
  15.2 8.4 %collective-permute-start.9 = (bf16[1040,128]{1,0:T(8,128)(2,1)S(1)}, bf16[1040,128]{1,0:T(8,128)(2,1)S(1)}, u32[]{:S(2)}, u32[]{:S(2)}) collective-permute-start(bf16[1040,128]{1,0:T(8,128)(2,1)S(1)} %collective-permute-done), channel_id=1, source_target_pairs={{0,1},{1,0},{2,3},{3,2},{4,6},{5,7},{6,4},{7,5},{8,9},{9,8},{10,11... | collective-permute-start | bytes 798728 | tf_op jit(solution)/shard_map/ppermute | solution.py:288
  15.3 8.5 %collective-permute-start.1 = (bf16[1040,128]{1,0:T(8,128)(2,1)S(1)}, bf16[1040,128]{1,0:T(8,128)(2,1)S(1)}, u32[]{:S(2)}, u32[]{:S(2)}) collective-permute-start(bf16[1040,128]{1,0:T(8,128)(2,1)S(1)} %collective-permute-done), channel_id=1, source_target_pairs={{0,8},{1,9},{2,10},{3,11},{4,12},{5,13},{6,14},{7,15},{8,24},{9,25... | collective-permute-start | bytes 798728 | tf_op jit(solution)/shard_map/ppermute | solution.py:288
  23.7 11.3 %collective-permute-start.10 = (bf16[2080,128]{1,0:T(8,128)(2,1)S(1)}, bf16[2080,128]{1,0:T(8,128)(2,1)S(1)}, u32[]{:S(2)}, u32[]{:S(2)}) collective-permute-start(bf16[2080,128]{1,0:T(8,128)(2,1)S(1)} %pad_maximum_fusion.3), channel_id=1, source_target_pairs={{0,2},{1,3},{2,0},{3,1},{4,5},{5,4},{6,7},{7,6},{8,10},{9,11},{10,... | collective-permute-start | bytes 1597448 | tf_op jit(solution)/shard_map/ppermute | solution.py:288
  23.8 7.5 %collective-permute-start.7 = (bf16[1040,128]{1,0:T(8,128)(2,1)S(1)}, bf16[1040,128]{1,0:T(8,128)(2,1)S(1)}, u32[]{:S(2)}, u32[]{:S(2)}) collective-permute-start(bf16[1040,128]{1,0:T(8,128)(2,1)S(1)} %collective-permute-done.1), channel_id=1, source_target_pairs={{0,1},{1,0},{2,3},{3,2},{4,6},{5,7},{6,4},{7,5},{8,9},{9,8},{10,11... | collective-permute-start | bytes 798728 | tf_op jit(solution)/shard_map/ppermute | solution.py:288
  25.1 10.0 %collective-permute-start.13 = (bf16[4160,128]{1,0:T(8,128)(2,1)S(1)}, bf16[4160,128]{1,0:T(8,128)(2,1)S(1)}, u32[]{:S(2)}, u32[]{:S(2)}) collective-permute-start(bf16[4160,128]{1,0:T(8,128)(2,1)S(1)} %constant_dynamic-update-slice_fusion.3.refs_0_), channel_id=1, source_target_pairs={{0,4},{1,5},{2,6},{3,7},{4,0},{5,1},{6,2},{7,3},{8,12},{9,13},{10,... | collective-permute-start | bytes 3194888 | tf_op jit(solution)/shard_map/ppermute | solution.py:288
  26.8 10.8 %collective-permute-start.2 = (bf16[1040,128]{1,0:T(8,128)(2,1)S(1)}, bf16[1040,128]{1,0:T(8,128)(2,1)S(1)}, u32[]{:S(2)}, u32[]{:S(2)}) collective-permute-start(bf16[1040,128]{1,0:T(8,128)(2,1)S(1)} %collective-permute-done.1), channel_id=1, source_target_pairs={{0,8},{1,9},{2,10},{3,11},{4,12},{5,13},{6,14},{7,15},{8,24},{9,25... | collective-permute-start | bytes 798728 | tf_op jit(solution)/shard_map/ppermute | solution.py:288
  31.3 9.5 %collective-permute-start.8 = (bf16[2080,128]{1,0:T(8,128)(2,1)S(1)}, bf16[2080,128]{1,0:T(8,128)(2,1)S(1)}, u32[]{:S(2)}, u32[]{:S(2)}) collective-permute-start(bf16[2080,128]{1,0:T(8,128)(2,1)S(1)} %pad_maximum_fusion.2), channel_id=1, source_target_pairs={{0,2},{1,3},{2,0},{3,1},{4,5},{5,4},{6,7},{7,6},{8,10},{9,11},{10,... | collective-permute-start | bytes 1597448 | tf_op jit(solution)/shard_map/ppermute | solution.py:288
  37.4 3.4 %collective-permute-start.14 = (bf16[4160,128]{1,0:T(8,128)(2,1)S(1)}, bf16[4160,128]{1,0:T(8,128)(2,1)S(1)}, u32[]{:S(2)}, u32[]{:S(2)}) collective-permute-start(bf16[4160,128]{1,0:T(8,128)(2,1)S(1)} %pad_maximum_fusion.1.refs_0_), channel_id=1, source_target_pairs={{0,4},{1,5},{2,6},{3,7},{4,0},{5,1},{6,2},{7,3},{8,12},{9,13},{10,... | collective-permute-start | bytes 3194888 | tf_op jit(solution)/shard_map/ppermute | solution.py:288
  37.6 10.9 %collective-permute-start.3 = (bf16[1040,128]{1,0:T(8,128)(2,1)S(1)}, bf16[1040,128]{1,0:T(8,128)(2,1)S(1)}, u32[]{:S(2)}, u32[]{:S(2)}) collective-permute-start(bf16[1040,128]{1,0:T(8,128)(2,1)S(1)} %collective-permute-done.2), channel_id=1, source_target_pairs={{0,1},{1,0},{2,3},{3,2},{4,6},{5,7},{6,4},{7,5},{8,9},{9,8},{10,11... | collective-permute-start | bytes 798728 | tf_op jit(solution)/shard_map/ppermute | solution.py:288
  38.0 10.5 %collective-permute-start.5 = (bf16[1040,128]{1,0:T(8,128)(2,1)S(1)}, bf16[1040,128]{1,0:T(8,128)(2,1)S(1)}, u32[]{:S(2)}, u32[]{:S(2)}) collective-permute-start(bf16[1040,128]{1,0:T(8,128)(2,1)S(1)} %collective-permute-done.2), channel_id=1, source_target_pairs={{0,2},{1,3},{2,0},{3,1},{4,5},{5,4},{6,7},{7,6},{8,10},{9,11},{10,... | collective-permute-start | bytes 798728 | tf_op jit(solution)/shard_map/ppermute | solution.py:288
  44.4 6.6 %collective-permute-start.15 = (bf16[4160,128]{1,0:T(8,128)(2,1)S(1)}, bf16[4160,128]{1,0:T(8,128)(2,1)S(1)}, u32[]{:S(2)}, u32[]{:S(2)}) collective-permute-start(bf16[4160,128]{1,0:T(8,128)(2,1)S(1)} %pad_maximum_fusion.refs_0_), channel_id=1, source_target_pairs={{0,4},{1,5},{2,6},{3,7},{4,0},{5,1},{6,2},{7,3},{8,12},{9,13},{10,... | collective-permute-start | bytes 3194888 | tf_op jit(solution)/shard_map/ppermute | solution.py:288
  48.6 6.5 %collective-permute-start.6 = (bf16[3120,128]{1,0:T(8,128)(2,1)S(1)}, bf16[3120,128]{1,0:T(8,128)(2,1)S(1)}, u32[]{:S(2)}, u32[]{:S(2)}) collective-permute-start(bf16[3120,128]{1,0:T(8,128)(2,1)S(1)} %constant_dynamic-update-slice_fusion.refs_0_), channel_id=1, source_target_pairs={{0,4},{1,5},{2,6},{3,7},{4,0},{5,1},{6,2},{7,3},{8,12},{9,13},{10,... | collective-permute-start | bytes 2396168 | tf_op jit(solution)/shard_map/ppermute | solution.py:288
  49.6 9.2 %collective-permute-start.4 = (bf16[1040,128]{1,0:T(8,128)(2,1)S(1)}, bf16[1040,128]{1,0:T(8,128)(2,1)S(1)}, u32[]{:S(2)}, u32[]{:S(2)}) collective-permute-start(bf16[1040,128]{1,0:T(8,128)(2,1)S(1)} %collective-permute-done.3), channel_id=1, source_target_pairs={{0,2},{1,3},{2,0},{3,1},{4,5},{5,4},{6,7},{7,6},{8,10},{9,11},{10,... | collective-permute-start | bytes 798728 | tf_op jit(solution)/shard_map/ppermute | solution.py:288
  58.8 1.6 %collective-permute-start.16 = (bf16[1040,128]{1,0:T(8,128)(2,1)S(1)}, bf16[1040,128]{1,0:T(8,128)(2,1)S(1)}, u32[]{:S(2)}, u32[]{:S(2)}) collective-permute-start(bf16[1040,128]{1,0:T(8,128)(2,1)S(1)} %collective-permute-done.4.refs_0_), channel_id=1, source_target_pairs={{0,4},{1,5},{2,6},{3,7},{4,0},{5,1},{6,2},{7,3},{8,12},{9,13},{10,... | collective-permute-start | bytes 798728 | tf_op jit(solution)/shard_map/ppermute | solution.py:288
where the time goes:
time: 65.5 us; the launch traced here: 64.6 us
  waiting for transfers between devices  22.7 us (35%)
  Pallas kernels  19.3 us (29%)
  starting transfers between devices  19.1 us (29%)
  local copies, waits for them, and re-layouts  2.32 us (4%)
  other arithmetic  0.96 us (1%)
    ppermute x17, waiting for transfers between devices, permute(): return lax.ppermute(x, AXES, pairs)  22.7 us
    pallas_call x7, Pallas kernels, call(): pl.pallas_call(kernel, out_shape=shapes, in_specs=[vmem] * len(operands),...  19.3 us
    ppermute x17, starting transfers between devices, permute(): return lax.ppermute(x, AXES, pairs)  19.1 us
    reshape x2, local copies, waits for them, and re-layouts, per_device(): x.reshape(2, RUN, heads_kv, head_dim)  1.94 us
  transfers between devices with their start and end apart: 17, of which 8 were waited for; matrix products, arithmetic and copies ran while one was open for 1% of the time, Pallas kernels for 23%

commit v1 on v0

--- a/solution.py
+++ b/solution.py
@@ -92,7 +92,7 @@
         head_tile(q_ref, state_refs, a, own, lambda h: own(heads_kv + h), factor, live)
 
 
-def attend_kernel(group, factor, half, last, blocks, q_ref, *refs):
+def attend_kernel(group, factor, half, last, keep, blocks, q_ref, *refs):
     heads_kv, rows, head_dim = q_ref.shape[1:]
     run_rows = 2 * heads_kv * RUN
     block_rows = 2 * run_rows + 16
@@ -100,7 +100,7 @@
     refs = refs[5:]
     if last:
         out_ref, refs = refs[0], refs[1:]
-    meta_ref, *state_refs, buf = refs
+    meta_ref, *state_refs, buf = refs[:5]
 
     meta = meta_ref[...]
     counts = tuple(
@@ -170,7 +170,7 @@
         count = jnp.where(a == 0, counts[0], counts[1])
         start = count // TILE * TILE
         runs = TILE // 2
-        while runs >= (1 if last else KEEP):
+        while runs >= keep:
 
             @pl.when(count & runs != 0)
             def _():
@@ -185,18 +185,21 @@
     if not last:
         row = lax.broadcasted_iota(jnp.int32, meta.shape, 0)
         for a in range(2):
-            start = counts[a] // KEEP * KEEP
+            start = counts[a] // keep * keep
             rest = counts[a] - start
-
-            @pl.when((start > 0) & (rest > 0))
-            def _():
-                for n in range(KEEP - 1):
-                    buf[a, n] = buf[a, start + n]
+            if keep > 1:
+
+                @pl.when((start > 0) & (rest > 0))
+                def _():
+                    for n in range(keep - 1):
+                        buf[a, n] = buf[a, start + n]
 
             meta = jnp.where(row == 2 + a, rest.astype(jnp.float32), meta)
         meta_ref[...] = meta
         return
 
+    made, sems = refs[5:]
+    copies = []
     for a in range(2):
         for h in range(0, heads_kv, 2):
             done = []
@@ -204,9 +207,45 @@
                 total = jnp.sum(state_refs[1][a, g], axis=1, keepdims=True)
                 part = state_refs[2][a, g] * (1.0 / total)
                 done.append(part.reshape(RUN, group, -1))
-            out_ref[a * RUN : (a + 1) * RUN, h * group : (h + 2) * group, :] = (
-                jnp.concatenate(done, axis=1).astype(out_ref.dtype)
+            place = (slice(a * RUN, (a + 1) * RUN), slice(h * group, (h + 2) * group))
+            made[place] = jnp.concatenate(done, axis=1).astype(out_ref.dtype)
+            copy = pltpu.make_async_copy(
+                made.at[place], out_ref.at[place], sems.at[len(copies)]
             )
+            copy.start()
+            copies.append(copy)
+    for copy in copies:
+        copy.wait()
+
+
+def pack_kernel(k_any, v_any, positions_any, own_ref, k_ref, v_ref, positions_ref, sems):
+    pairs = ((k_any, k_ref), (v_any, v_ref), (positions_any, positions_ref))
+    copies = [
+        pltpu.make_async_copy(source, target, sems.at[n])
+        for n, (source, target) in enumerate(pairs)
+    ]
+    for copy in copies:
+        copy.start()
+    heads_kv = k_ref.shape[0] // (2 * RUN)
+    rows = heads_kv * RUN
+    at = lax.broadcasted_iota(jnp.int32, (rows, rows), 0)
+    origin = lax.broadcasted_iota(jnp.int32, (rows, rows), 1)
+    move = at % RUN * heads_kv + at // RUN == origin
+    move = jnp.where(move, 1.0, 0.0).astype(k_ref.dtype)
+    for n, ref in enumerate((k_ref, v_ref)):
+        copies[n].wait()
+        for r in range(2):
+            moved = jnp.dot(
+                move,
+                ref[r * rows : (r + 1) * rows],
+                preferred_element_type=jnp.float32,
+            )
+            start = (2 * r + n) * rows
+            own_ref[start : start + rows] = moved.astype(own_ref.dtype)
+    copies[2].wait()
+    numbers = (positions_ref[...] // RUN).astype(jnp.float32)
+    numbers = jnp.broadcast_to(numbers, (16, numbers.shape[1]))
+    own_ref[4 * rows :] = numbers.astype(own_ref.dtype)
 
 
 class Attention:
@@ -225,13 +264,20 @@
             jax.ShapeDtypeStruct((2, slots, 2 * heads_kv * RUN, head_dim), q.dtype)
         )
 
-    def call(self, kernel, operands, shapes, aliases, count, name):
+    def call(self, kernel, operands, shapes, aliases, count, name, out=None):
         vmem = pl.BlockSpec(memory_space=pltpu.VMEM)
+        out_specs = [vmem] * len(shapes)
+        scratch = []
+        if out is not None:
+            shapes = [out, *shapes]
+            out_specs.insert(0, pl.BlockSpec(memory_space=pl.ANY))
+            scratch = [pltpu.VMEM(out.shape, out.dtype), pltpu.SemaphoreType.DMA((8,))]
         return pl.pallas_call(
             kernel,
             out_shape=shapes,
             in_specs=[vmem] * len(operands),
-            out_specs=[vmem] * len(shapes),
+            out_specs=out_specs,
+            scratch_shapes=scratch,
             input_output_aliases=aliases,
             compiler_params=pltpu.CompilerParams(vmem_limit_bytes=28 * 1024 * 1024),
             cost_estimate=pl.CostEstimate(
@@ -246,18 +292,17 @@
         kernel = functools.partial(own_kernel, self.group, self.factor, self.half)
         return self.call(kernel, [self.q, own], self.carried, {}, 2, "attend_own")
 
-    def add(self, state, kvs, out=None):
+    def add(self, state, kvs, keep=KEEP, out=None):
         kvs = [x if isinstance(x, tuple) else (x, 0) for x in kvs]
         blocks = [(skip, x.shape[0] // self.block_rows) for x, skip in kvs]
         count = sum(end - skip for skip, end in blocks)
         operands = [self.q, *(x for x, _ in kvs), *state]
         first, ahead = 1 + len(kvs), int(out is not None)
         aliases = {first + n: ahead + n for n in range(len(state))}
-        shapes = ([out] if ahead else []) + self.carried
         kernel = functools.partial(
-            attend_kernel, self.group, self.factor, self.half, out is not None, blocks
+            attend_kernel, self.group, self.factor, self.half, ahead, keep, blocks
         )
-        results = self.call(kernel, operands, shapes, aliases, count, "attend")
+        results = self.call(kernel, operands, self.carried, aliases, count, "attend", out)
         return results[0] if ahead else results
 
 
@@ -302,16 +347,23 @@
     def tied(x, *others):
         return lax.optimization_barrier((x, *others))[0]
 
-    by_run = jnp.concatenate(
-        [x.reshape(2, RUN, heads_kv, head_dim) for x in (keys, values)], axis=2
-    ).transpose(0, 2, 1, 3)
-    numbers = (positions // RUN).astype(jnp.bfloat16)
-    own = jnp.concatenate(
-        [
-            by_run.reshape(-1, head_dim),
-            jnp.broadcast_to(numbers[None, :], (16, head_dim)),
-        ]
-    )
+    flat = jax.ShapeDtypeStruct((tokens * heads_kv, head_dim), keys.dtype)
+    own = pl.pallas_call(
+        pack_kernel,
+        out_shape=jax.ShapeDtypeStruct(
+            (2 * tokens * heads_kv + 16, head_dim), keys.dtype
+        ),
+        in_specs=[pl.BlockSpec(memory_space=pltpu.HBM)] * 3,
+        out_specs=pl.BlockSpec(memory_space=pltpu.VMEM),
+        scratch_shapes=[
+            pltpu.VMEM(flat.shape, flat.dtype),
+            pltpu.VMEM(flat.shape, flat.dtype),
+            pltpu.VMEM((1, tokens), jnp.int32),
+            pltpu.SemaphoreType.DMA((3,)),
+        ],
+        compiler_params=pltpu.CompilerParams(vmem_limit_bytes=60 * 1024 * 1024),
+        name="pack",
+    )(keys.reshape(flat.shape), values.reshape(flat.shape), positions.reshape(1, tokens))
     q = (
         queries.reshape(2, RUN, heads_kv, group, head_dim)
         .transpose(0, 2, 1, 3, 4)
@@ -321,33 +373,53 @@
     attention = Attention(q, group, half, 2 * inner)
     state = attention.start(own)
 
-    stage, waiting = own, None
-    for n in range(chips - 1):
-        following = along_z(stage)
-        held = stage
+    single = [1 << step for step in range(bits)]
+    several = [m for m in range(1, inner) if m not in single]
+
+    stages = [own]
+    for n in range(1, chips):
+        stages.append(along_z(stages[-1]))
+    planes, ready = [], []
+    for n in range(chips):
+        stage = stages[n]
+        before = planes[n - 1] if n else {}
+        if n:
+            earlier = [before[m] for m in single]
+            if n > 1:
+                earlier += [planes[n - 2][m] for m in several]
+            if n > 2:
+                state = attention.add(state, ready[n - 3])
+                earlier.append(state[0])
+            stage = tied(stage, *earlier)
+        found = {0: stage}
         for step in range(bits):
-            if n == 0 and step == 1:
-                held = tied(held, following, state[0])
-            held = jnp.concatenate([held, over_place(held, step)])
-        if waiting:
-            state = attention.add(state, waiting)
-            held = tied(held, state[0])
-        waiting = [(held, int(n == 0)), other_core(held)]
-        stage = following
-
-    found = [stage]
-    for step in range(bits):
-        found += [over_place(x, step) for x in found]
-    *most, final = found
+            found[1 << step] = over_place(stage, step)
+        if n + 1 < chips:
+            wait_for = [stages[n + 1]] + ([state[0]] if n == 0 else [])
+        else:
+            state = attention.add(state, ready[n - 2])
+            wait_for = [state[0]]
+        for m in several:
+            if n + 2 == chips:
+                found[m] = along_z(tied(before[m], *wait_for))
+            else:
+                top = m.bit_length() - 1
+                found[m] = over_place(tied(found[m - (1 << top)], *wait_for), top)
+        planes.append(found)
+        if n + 1 < chips:
+            held = jnp.concatenate([found[m] for m in range(inner)])
+            ready.append([(held, int(n == 0)), other_core(held)])
+    waiting = ready[-1]
+    *most, final = (found[m] for m in range(inner))
     most = jnp.concatenate(most)
     theirs = other_core(most)
     state = attention.add(state, waiting)
     state = attention.add(state, [most, theirs])
     final = tied(final, state[0])
     theirs = other_core(final)
-    state = attention.add(state, [final])
+    state = attention.add(state, [final], keep=1)
     out = jax.ShapeDtypeStruct(queries.shape, queries.dtype)
-    return attention.add(state, [theirs], out)
+    return attention.add(state, [theirs], keep=1, out=out)
 
 
 def solution(mesh):

time: 65.5 us -> 70.8 us (1.081)
  waiting for transfers between devices: 22.7 us -> 26.9 us
  starting transfers between devices: 19.1 us -> 20.7 us
  other arithmetic: 0.96 us -> 0.07 us
    ppermute x17 -> x20, waiting for transfers between devices: 22.7 us -> 26.9 us  [permute(): return lax.ppermute(x, AXES, pairs)]
    pallas_call x0 -> x1, Pallas kernels: none -> 2.08 us  [per_device(): pl.pallas_call(pack_kernel, out_shape=jax.ShapeDtypeStruct((2 * tokens *...]
    reshape x2 -> x0, local copies, waits for them, and re-layouts: 1.94 us -> none  [per_device(): x.reshape(2, RUN, heads_kv, head_dim)]
    pallas_call x7, Pallas kernels: 19.3 us -> 17.7 us  [call(): pl.pallas_call(kernel, out_shape=shapes, in_specs=[vmem] * len(operands),...]
    ppermute x17 -> x20, starting transfers between devices: 19.1 us -> 20.7 us  [permute(): return lax.ppermute(x, AXES, pairs)]
    reshape x1, local copies, waits for them, and re-layouts: 0.18 us -> 1.41 us  [per_device(): queries.reshape(2, RUN, heads_kv, group, head_dim).transpose(0, 2, 1, 3, 4)]
  transfers between devices with their start and end apart: 17 -> 20, of which waited for: 8 -> 9; matrix products, arithmetic and copies ran while one was open for 1% -> 3% of each run, Pallas kernels for 23% -> 22%
where the time goes in v1:
time: 70.8 us; the launch traced here: 69.6 us
  waiting for transfers between devices  26.9 us (38%)
  starting transfers between devices  20.7 us (29%)
  Pallas kernels  19.8 us (28%)
  local copies, waits for them, and re-layouts  1.76 us (2%)
    ppermute x20, waiting for transfers between devices, permute(): return lax.ppermute(x, AXES, pairs)  26.9 us
    ppermute x20, starting transfers between devices, permute(): return lax.ppermute(x, AXES, pairs)  20.7 us
    pallas_call x7, Pallas kernels, call(): pl.pallas_call(kernel, out_shape=shapes, in_specs=[vmem] * len(operands),...  17.7 us
    pallas_call x1, Pallas kernels, per_device(): pl.pallas_call(pack_kernel, out_shape=jax.ShapeDtypeStruct((2 * tokens *...  2.08 us
  transfers between devices with their start and end apart: 20, of which 9 were waited for; matrix products, arithmetic and copies ran while one was open for 3% of the time, Pallas kernels for 22%

profile of v1, /device:TPU:1, one launch (start us, length us, event | category | flops | bytes accessed | tf_op | source)
XLA Modules:
  0.0 69.6 jit_solution(7302195740335759345)
XLA Ops:
  0.0 2.1 %pack.1.own_ref = bf16[1040,128]{1,0:T(8,128)(2,1)} custom-call(bf16[512,128]{1,0:T(8,128)(2,1)} %bitcast.17, bf16[512,128]{1,0:T(8,128)(2,1)} %bitcast.18, s32[1,128]{1,0:T(1,128)} %bitcast.19), custom_call_target="tpu_custom_call" | custom-call | tf_op jit(solution)/shard_map/pack/pallas_call | solution.py:351
  2.1 0.0 copy-start
  2.1 2.2 %collective-permute-start = (bf16[1040,128]{1,0:T(8,128)(2,1)}, bf16[1040,128]{1,0:T(8,128)(2,1)S(1)}, u32[]{:S(2)}, u32[]{:S(2)}) collective-permute-start(bf16[1040,128]{1,0:T(8,128)(2,1)} %pack.1.own_ref), channel_id=1, source_target_pairs={{0,8},{1,9},{2,10},{3,11},{4,12},{5,13},{6,14},{7,15},{8,24},{9,25... | collective-permute-start | bytes 798728 | tf_op jit(solution)/shard_map/ppermute | solution.py:333
  4.3 1.2 %collective-permute-start.3 = (bf16[1040,128]{1,0:T(8,128)(2,1)}, bf16[1040,128]{1,0:T(8,128)(2,1)S(1)}, u32[]{:S(2)}, u32[]{:S(2)}) collective-permute-start(bf16[1040,128]{1,0:T(8,128)(2,1)} %pack.1.own_ref), channel_id=1, source_target_pairs={{0,1},{1,0},{2,3},{3,2},{4,6},{5,7},{6,4},{7,5},{8,9},{9,8},{10,11... | collective-permute-start | bytes 798728 | tf_op jit(solution)/shard_map/ppermute | solution.py:333
  5.5 1.2 %collective-permute-start.4 = (bf16[1040,128]{1,0:T(8,128)(2,1)}, bf16[1040,128]{1,0:T(8,128)(2,1)S(1)}, u32[]{:S(2)}, u32[]{:S(2)}) collective-permute-start(bf16[1040,128]{1,0:T(8,128)(2,1)} %pack.1.own_ref), channel_id=1, source_target_pairs={{0,2},{1,3},{2,0},{3,1},{4,5},{5,4},{6,7},{7,6},{8,10},{9,11},{10,... | collective-permute-start | bytes 798728 | tf_op jit(solution)/shard_map/ppermute | solution.py:333
  6.7 1.4 %copy.37 = bf16[2,64,4,8,128]{4,3,1,2,0:T(8,128)(2,1)S(1)} copy(bf16[2,64,4,8,128]{4,3,2,1,0:T(8,128)(2,1)} %bitcast.16) | data formatting | bytes 2097152 | tf_op jit(solution)/shard_map/reshape | solution.py:368
  8.2 1.2 %attend_own.1 = (f32[8,128]{1,0:T(8,128)S(1)}, f32[2,4,512,128]{3,2,1,0:T(8,128)S(1)}, f32[2,4,512,128]{3,2,1,0:T(8,128)S(1)}, f32[2,4,512,128]{3,2,1,0:T(8,128)S(1)}, bf16[2,20,512,128]{3,2,1,0:T(8,128)(2,1)S(1)}) custom-call(bf16[2,4,512,128]{3,2,1,0:T(8,128)(2,1)S(1)} %bitcast.9, bf16[1040,128]{1,0:T(8,128)(2,1)S(1)} %copy-done), custom_call_target="tpu_custom_call" | custom-call | flops 268435456 | bytes 4194304 | tf_op jit(solution)/shard_map/attend_own/pallas_call | solution.py:275
  9.3 2.3 %collective-permute-done = bf16[1040,128]{1,0:T(8,128)(2,1)S(1)} collective-permute-done((bf16[1040,128]{1,0:T(8,128)(2,1)}, bf16[1040,128]{1,0:T(8,128)(2,1)S(1)}, u32[]{:S(2)}, u32[]{:S(2)}) %collective-permute-start) | collective-permute-done | bytes 266272 | tf_op jit(solution)/shard_map/ppermute | solution.py:333
  11.6 0.0 collective-permute-done.3
  11.6 2.3 %collective-permute-done.4 = bf16[1040,128]{1,0:T(8,128)(2,1)S(1)} collective-permute-done((bf16[1040,128]{1,0:T(8,128)(2,1)}, bf16[1040,128]{1,0:T(8,128)(2,1)S(1)}, u32[]{:S(2)}, u32[]{:S(2)}) %collective-permute-start.4) | collective-permute-done | bytes 266272 | tf_op jit(solution)/shard_map/ppermute | solution.py:333
  14.0 0.0 collective-permute-start.5
  14.0 1.2 %collective-permute-start.6 = (bf16[1040,128]{1,0:T(8,128)(2,1)S(1)}, bf16[1040,128]{1,0:T(8,128)(2,1)S(1)}, u32[]{:S(2)}, u32[]{:S(2)}) collective-permute-start(bf16[1040,128]{1,0:T(8,128)(2,1)S(1)} %collective-permute-done), channel_id=1, source_target_pairs={{0,2},{1,3},{2,0},{3,1},{4,5},{5,4},{6,7},{7,6},{8,10},{9,11},{10,... | collective-permute-start | bytes 798728 | tf_op jit(solution)/shard_map/ppermute | solution.py:333
  15.2 2.3 %collective-permute-start.1 = (bf16[1040,128]{1,0:T(8,128)(2,1)S(1)}, bf16[1040,128]{1,0:T(8,128)(2,1)S(1)}, u32[]{:S(2)}, u32[]{:S(2)}) collective-permute-start(bf16[1040,128]{1,0:T(8,128)(2,1)S(1)} %collective-permute-done), channel_id=1, source_target_pairs={{0,8},{1,9},{2,10},{3,11},{4,12},{5,13},{6,14},{7,15},{8,24},{9,25... | collective-permute-start | bytes 798728 | tf_op jit(solution)/shard_map/ppermute | solution.py:333
  17.5 0.3 collective-permute-start.7
  17.8 4.8 %collective-permute-done.1 = bf16[1040,128]{1,0:T(8,128)(2,1)S(1)} collective-permute-done((bf16[1040,128]{1,0:T(8,128)(2,1)S(1)}, bf16[1040,128]{1,0:T(8,128)(2,1)S(1)}, u32[]{:S(2)}, u32[]{:S(2)}) %collective-permute-start.1) | collective-permute-done | bytes 266272 | tf_op jit(solution)/shard_map/ppermute | solution.py:333
  22.6 0.0 collective-permute-done.5
  22.6 0.0 collective-permute-done.6
  22.6 2.6 %collective-permute-done.7 = bf16[1040,128]{1,0:T(8,128)(2,1)S(1)} collective-permute-done((bf16[1040,128]{1,0:T(8,128)(2,1)S(1)}, bf16[1040,128]{1,0:T(8,128)(2,1)S(1)}, u32[]{:S(2)}, u32[]{:S(2)}) %collective-permute-start.7) | collective-permute-done | bytes 266272 | tf_op jit(solution)/shard_map/ppermute | solution.py:333
  25.2 1.2 %collective-permute-start.8 = (bf16[1040,128]{1,0:T(8,128)(2,1)S(1)}, bf16[1040,128]{1,0:T(8,128)(2,1)S(1)}, u32[]{:S(2)}, u32[]{:S(2)}) collective-permute-start(bf16[1040,128]{1,0:T(8,128)(2,1)S(1)} %collective-permute-done.1), channel_id=1, source_target_pairs={{0,1},{1,0},{2,3},{3,2},{4,6},{5,7},{6,4},{7,5},{8,9},{9,8},{10,11... | collective-permute-start | bytes 798728 | tf_op jit(solution)/shard_map/ppermute | solution.py:333
  26.4 1.0 %collective-permute-start.9 = (bf16[1040,128]{1,0:T(8,128)(2,1)S(1)}, bf16[1040,128]{1,0:T(8,128)(2,1)S(1)}, u32[]{:S(2)}, u32[]{:S(2)}) collective-permute-start(bf16[1040,128]{1,0:T(8,128)(2,1)S(1)} %collective-permute-done.1), channel_id=1, source_target_pairs={{0,2},{1,3},{2,0},{3,1},{4,5},{5,4},{6,7},{7,6},{8,10},{9,11},{10,... | collective-permute-start | bytes 798728 | tf_op jit(solution)/shard_map/ppermute | solution.py:333
  27.4 0.5 collective-permute-start.10
  28.0 0.1 pad_maximum_fusion.refs_0_
  28.0 1.3 %collective-permute-start.11 = (bf16[4160,128]{1,0:T(8,128)(2,1)S(1)}, bf16[4160,128]{1,0:T(8,128)(2,1)S(1)}, u32[]{:S(2)}, u32[]{:S(2)}) collective-permute-start(bf16[4160,128]{1,0:T(8,128)(2,1)S(1)} %pad_maximum_fusion.refs_0_), channel_id=1, source_target_pairs={{0,4},{1,5},{2,6},{3,7},{4,0},{5,1},{6,2},{7,3},{8,12},{9,13},{10,... | collective-permute-start | bytes 3194888 | tf_op jit(solution)/shard_map/ppermute | solution.py:333
  29.4 2.3 %collective-permute-start.2 = (bf16[1040,128]{1,0:T(8,128)(2,1)S(1)}, bf16[1040,128]{1,0:T(8,128)(2,1)S(1)}, u32[]{:S(2)}, u32[]{:S(2)}) collective-permute-start(bf16[1040,128]{1,0:T(8,128)(2,1)S(1)} %collective-permute-done.1), channel_id=1, source_target_pairs={{0,8},{1,9},{2,10},{3,11},{4,12},{5,13},{6,14},{7,15},{8,24},{9,25... | collective-permute-start | bytes 798728 | tf_op jit(solution)/shard_map/ppermute | solution.py:333
  31.8 5.6 %collective-permute-done.10 = bf16[1040,128]{1,0:T(8,128)(2,1)S(1)} collective-permute-done((bf16[1040,128]{1,0:T(8,128)(2,1)S(1)}, bf16[1040,128]{1,0:T(8,128)(2,1)S(1)}, u32[]{:S(2)}, u32[]{:S(2)}) %collective-permute-start.10) | collective-permute-done | bytes 266272 | tf_op jit(solution)/shard_map/ppermute | solution.py:333
  37.4 0.1 collective-permute-start.13
  37.5 0.8 %collective-permute-done.2 = bf16[1040,128]{1,0:T(8,128)(2,1)S(1)} collective-permute-done((bf16[1040,128]{1,0:T(8,128)(2,1)S(1)}, bf16[1040,128]{1,0:T(8,128)(2,1)S(1)}, u32[]{:S(2)}, u32[]{:S(2)}) %collective-permute-start.2) | collective-permute-done | bytes 266272 | tf_op jit(solution)/shard_map/ppermute | solution.py:333
  38.2 1.6 %collective-permute-start.17 = (bf16[1040,128]{1,0:T(8,128)(2,1)S(1)}, bf16[1040,128]{1,0:T(8,128)(2,1)S(1)}, u32[]{:S(2)}, u32[]{:S(2)}) collective-permute-start(bf16[1040,128]{1,0:T(8,128)(2,1)S(1)} %collective-permute-done.10), channel_id=1, source_target_pairs={{0,8},{1,9},{2,10},{3,11},{4,12},{5,13},{6,14},{7,15},{8,24},{9,25... | collective-permute-start | bytes 798728 | tf_op jit(solution)/shard_map/ppermute | solution.py:333
  39.8 0.0 collective-permute-done.8
  39.9 0.0 collective-permute-done.9
  39.9 0.0 collective-permute-done.11.refs_1_
  40.0 2.9 %attend.6 = (f32[8,128]{1,0:T(8,128)S(1)}, f32[2,4,512,128]{3,2,1,0:T(8,128)S(1)}, f32[2,4,512,128]{3,2,1,0:T(8,128)S(1)}, f32[2,4,512,128]{3,2,1,0:T(8,128)S(1)}, bf16[2,20,512,128]{3,2,1,0:T(8,128)(2,1)S(1)}) custom-call(bf16[2,4,512,128]{3,2,1,0:T(8,128)(2,1)S(1)} %bitcast.10, ...), custom_call_target="tpu_custom_call", output_to_operand_aliasing={{0}: (3, {}), {1}: (4, {}), {2}: (5, {}), {3}: (6, {}), {4}... | custom-call | flops 939524096 | bytes 4194304 | tf_op jit(solution)/shard_map/attend/pallas_call | solution.py:275
  42.8 0.1 collective-permute-start.12
  42.9 3.3 %collective-permute-done.17 = bf16[1040,128]{1,0:T(8,128)(2,1)S(1)} collective-permute-done((bf16[1040,128]{1,0:T(8,128)(2,1)S(1)}, bf16[1040,128]{1,0:T(8,128)(2,1)S(1)}, u32[]{:S(2)}, u32[]{:S(2)}) %collective-permute-start.17) | collective-permute-done | bytes 266272 | tf_op jit(solution)/shard_map/ppermute | solution.py:333
  46.2 1.8 %collective-permute-start.18 = (bf16[4160,128]{1,0:T(8,128)(2,1)S(1)}, bf16[4160,128]{1,0:T(8,128)(2,1)S(1)}, u32[]{:S(2)}, u32[]{:S(2)}) collective-permute-start(bf16[4160,128]{1,0:T(8,128)(2,1)S(1)} %constant_dynamic-update-slice_fusion.7.refs_0_), channel_id=1, source_target_pairs={{0,4},{1,5},{2,6},{3,7},{4,0},{5,1},{6,2},{7,3},{8,12},{9,13},{10,... | collective-permute-start | bytes 3194888 | tf_op jit(solution)/shard_map/ppermute | solution.py:333
  48.0 0.5 collective-permute-start.15
  48.6 5.0 %collective-permute-done.15 = bf16[1040,128]{1,0:T(8,128)(2,1)S(1)} collective-permute-done((bf16[1040,128]{1,0:T(8,128)(2,1)S(1)}, bf16[1040,128]{1,0:T(8,128)(2,1)S(1)}, u32[]{:S(2)}, u32[]{:S(2)}) %collective-permute-start.15) | collective-permute-done | bytes 266272 | tf_op jit(solution)/shard_map/ppermute | solution.py:333
  53.6 1.0 %collective-permute-start.16 = (bf16[3120,128]{1,0:T(8,128)(2,1)S(1)}, bf16[3120,128]{1,0:T(8,128)(2,1)S(1)}, u32[]{:S(2)}, u32[]{:S(2)}) collective-permute-start(bf16[3120,128]{1,0:T(8,128)(2,1)S(1)} %constant_dynamic-update-slice_fusion.4.refs_0_), channel_id=1, source_target_pairs={{0,4},{1,5},{2,6},{3,7},{4,0},{5,1},{6,2},{7,3},{8,12},{9,13},{10,... | collective-permute-start | bytes 2396168 | tf_op jit(solution)/shard_map/ppermute | solution.py:333
  54.6 3.4 %attend.7 = (f32[8,128]{1,0:T(8,128)S(1)}, f32[2,4,512,128]{3,2,1,0:T(8,128)S(1)}, f32[2,4,512,128]{3,2,1,0:T(8,128)S(1)}, f32[2,4,512,128]{3,2,1,0:T(8,128)S(1)}, bf16[2,20,512,128]{3,2,1,0:T(8,128)(2,1)S(1)}) custom-call(bf16[2,4,512,128]{3,2,1,0:T(8,128)(2,1)S(1)} %bitcast.11, ...), custom_call_target="tpu_custom_call", output_to_operand_aliasing={{0}: (3, {}), {1}: (4, {}), {2}: (5, {}), {3}: (6, {}), {4}... | custom-call | flops 1073741824 | bytes 4194304 | tf_op jit(solution)/shard_map/attend/pallas_call | solution.py:275
  58.1 0.7 %collective-permute-start.14 = (bf16[1040,128]{1,0:T(8,128)(2,1)S(1)}, bf16[1040,128]{1,0:T(8,128)(2,1)S(1)}, u32[]{:S(2)}, u32[]{:S(2)}) collective-permute-start(bf16[1040,128]{1,0:T(8,128)(2,1)S(1)} %collective-permute-done.12), channel_id=1, source_target_pairs={{0,2},{1,3},{2,0},{3,1},{4,5},{5,4},{6,7},{7,6},{8,10},{9,11},{10,... | collective-permute-start | bytes 798728 | tf_op jit(solution)/shard_map/ppermute | solution.py:333
  58.8 0.0 collective-permute-done.18.refs_1_
  58.8 3.7 %attend.8 = (f32[8,128]{1,0:T(8,128)S(1)}, f32[2,4,512,128]{3,2,1,0:T(8,128)S(1)}, f32[2,4,512,128]{3,2,1,0:T(8,128)S(1)}, f32[2,4,512,128]{3,2,1,0:T(8,128)S(1)}, bf16[2,20,512,128]{3,2,1,0:T(8,128)(2,1)S(1)}) custom-call(bf16[2,4,512,128]{3,2,1,0:T(8,128)(2,1)S(1)} %bitcast.12, ...), custom_call_target="tpu_custom_call", output_to_operand_aliasing={{0}: (3, {}), {1}: (4, {}), {2}: (5, {}), {3}: (6, {}), {4}... | custom-call | flops 1073741824 | bytes 4194304 | tf_op jit(solution)/shard_map/attend/pallas_call | solution.py:275
  62.5 2.8 %attend.9 = (f32[8,128]{1,0:T(8,128)S(1)}, f32[2,4,512,128]{3,2,1,0:T(8,128)S(1)}, f32[2,4,512,128]{3,2,1,0:T(8,128)S(1)}, f32[2,4,512,128]{3,2,1,0:T(8,128)S(1)}, bf16[2,20,512,128]{3,2,1,0:T(8,128)(2,1)S(1)}) custom-call(bf16[2,4,512,128]{3,2,1,0:T(8,128)(2,1)S(1)} %bitcast.13, ...), custom_call_target="tpu_custom_call", output_to_operand_aliasing={{0}: (3, {}), {1}: (4, {}), {2}: (5, {}), {3}: (6, {}), {4}... | custom-call | flops 805306368 | bytes 4194304 | tf_op jit(solution)/shard_map/attend/pallas_call | solution.py:275
  65.3 0.0 collective-permute-done.14.refs_0_
  65.3 0.1 collective-permute-start.19
  65.4 1.3 %attend.10 = (f32[8,128]{1,0:T(8,128)S(1)}, f32[2,4,512,128]{3,2,1,0:T(8,128)S(1)}, f32[2,4,512,128]{3,2,1,0:T(8,128)S(1)}, f32[2,4,512,128]{3,2,1,0:T(8,128)S(1)}, bf16[2,20,512,128]{3,2,1,0:T(8,128)(2,1)S(1)}) custom-call(bf16[2,4,512,128]{3,2,1,0:T(8,128)(2,1)S(1)} %bitcast.14, ...), custom_call_target="tpu_custom_call", output_to_operand_aliasing={{0}: (2, {}), {1}: (3, {}), {2}: (4, {}), {3}: (5, {}), {4}... | custom-call | flops 134217728 | bytes 4194304 | tf_op jit(solution)/shard_map/attend/pallas_call | solution.py:275
  66.8 0.2 collective-permute-done.19.refs_0_
  66.9 2.4 %attend.11 = (bf16[128,32,128]{2,1,0:T(8,128)(2,1)}, f32[8,128]{1,0:T(8,128)S(1)}, f32[2,4,512,128]{3,2,1,0:T(8,128)S(1)}, f32[2,4,512,128]{3,2,1,0:T(8,128)S(1)...) custom-call(bf16[2,4,512,128]{3,2,1,0:T(8,128)(2,1)S(1)} %bitcast.15, ...), custom_call_target="tpu_custom_call", output_to_operand_aliasing={{1}: (2, {}), {2}: (3, {}), {3}: (4, {}), {4}: (5, {}), {5}... | custom-call | flops 134217728 | bytes 4194304 | tf_op jit(solution)/shard_map/attend/pallas_call | solution.py:275
  (15 shorter events, 0.4 us)
Async XLA Ops:
  2.1 6.1 %copy-start = (bf16[1040,128]{1,0:T(8,128)(2,1)S(1)}, bf16[1040,128]{1,0:T(8,128)(2,1)}, u32[]{:S(2)}) copy-start(bf16[1040,128]{1,0:T(8,128)(2,1)} %pack.1.own_ref) | copy-start | bytes 798724
  2.1 9.5 %collective-permute-start = (bf16[1040,128]{1,0:T(8,128)(2,1)}, bf16[1040,128]{1,0:T(8,128)(2,1)S(1)}, u32[]{:S(2)}, u32[]{:S(2)}) collective-permute-start(bf16[1040,128]{1,0:T(8,128)(2,1)} %pack.1.own_ref), channel_id=1, source_target_pairs={{0,8},{1,9},{2,10},{3,11},{4,12},{5,13},{6,14},{7,15},{8,24},{9,25... | collective-permute-start | bytes 798728 | tf_op jit(solution)/shard_map/ppermute | solution.py:333
  4.3 7.4 %collective-permute-start.3 = (bf16[1040,128]{1,0:T(8,128)(2,1)}, bf16[1040,128]{1,0:T(8,128)(2,1)S(1)}, u32[]{:S(2)}, u32[]{:S(2)}) collective-permute-start(bf16[1040,128]{1,0:T(8,128)(2,1)} %pack.1.own_ref), channel_id=1, source_target_pairs={{0,1},{1,0},{2,3},{3,2},{4,6},{5,7},{6,4},{7,5},{8,9},{9,8},{10,11... | collective-permute-start | bytes 798728 | tf_op jit(solution)/shard_map/ppermute | solution.py:333
  5.5 8.4 %collective-permute-start.4 = (bf16[1040,128]{1,0:T(8,128)(2,1)}, bf16[1040,128]{1,0:T(8,128)(2,1)S(1)}, u32[]{:S(2)}, u32[]{:S(2)}) collective-permute-start(bf16[1040,128]{1,0:T(8,128)(2,1)} %pack.1.own_ref), channel_id=1, source_target_pairs={{0,2},{1,3},{2,0},{3,1},{4,5},{5,4},{6,7},{7,6},{8,10},{9,11},{10,... | collective-permute-start | bytes 798728 | tf_op jit(solution)/shard_map/ppermute | solution.py:333
  14.0 8.6 %collective-permute-start.5 = (bf16[1040,128]{1,0:T(8,128)(2,1)S(1)}, bf16[1040,128]{1,0:T(8,128)(2,1)S(1)}, u32[]{:S(2)}, u32[]{:S(2)}) collective-permute-start(bf16[1040,128]{1,0:T(8,128)(2,1)S(1)} %collective-permute-done), channel_id=1, source_target_pairs={{0,1},{1,0},{2,3},{3,2},{4,6},{5,7},{6,4},{7,5},{8,9},{9,8},{10,11... | collective-permute-start | bytes 798728 | tf_op jit(solution)/shard_map/ppermute | solution.py:333
  14.0 8.6 %collective-permute-start.6 = (bf16[1040,128]{1,0:T(8,128)(2,1)S(1)}, bf16[1040,128]{1,0:T(8,128)(2,1)S(1)}, u32[]{:S(2)}, u32[]{:S(2)}) collective-permute-start(bf16[1040,128]{1,0:T(8,128)(2,1)S(1)} %collective-permute-done), channel_id=1, source_target_pairs={{0,2},{1,3},{2,0},{3,1},{4,5},{5,4},{6,7},{7,6},{8,10},{9,11},{10,... | collective-permute-start | bytes 798728 | tf_op jit(solution)/shard_map/ppermute | solution.py:333
  15.2 7.4 %collective-permute-start.1 = (bf16[1040,128]{1,0:T(8,128)(2,1)S(1)}, bf16[1040,128]{1,0:T(8,128)(2,1)S(1)}, u32[]{:S(2)}, u32[]{:S(2)}) collective-permute-start(bf16[1040,128]{1,0:T(8,128)(2,1)S(1)} %collective-permute-done), channel_id=1, source_target_pairs={{0,8},{1,9},{2,10},{3,11},{4,12},{5,13},{6,14},{7,15},{8,24},{9,25... | collective-permute-start | bytes 798728 | tf_op jit(solution)/shard_map/ppermute | solution.py:333
  17.5 7.7 %collective-permute-start.7 = (bf16[1040,128]{1,0:T(8,128)(2,1)S(1)}, bf16[1040,128]{1,0:T(8,128)(2,1)S(1)}, u32[]{:S(2)}, u32[]{:S(2)}) collective-permute-start(bf16[1040,128]{1,0:T(8,128)(2,1)S(1)} %collective-permute-done.3), channel_id=1, source_target_pairs={{0,2},{1,3},{2,0},{3,1},{4,5},{5,4},{6,7},{7,6},{8,10},{9,11},{10,... | collective-permute-start | bytes 798728 | tf_op jit(solution)/shard_map/ppermute | solution.py:333
  25.2 14.6 %collective-permute-start.8 = (bf16[1040,128]{1,0:T(8,128)(2,1)S(1)}, bf16[1040,128]{1,0:T(8,128)(2,1)S(1)}, u32[]{:S(2)}, u32[]{:S(2)}) collective-permute-start(bf16[1040,128]{1,0:T(8,128)(2,1)S(1)} %collective-permute-done.1), channel_id=1, source_target_pairs={{0,1},{1,0},{2,3},{3,2},{4,6},{5,7},{6,4},{7,5},{8,9},{9,8},{10,11... | collective-permute-start | bytes 798728 | tf_op jit(solution)/shard_map/ppermute | solution.py:333
  26.4 13.5 %collective-permute-start.9 = (bf16[1040,128]{1,0:T(8,128)(2,1)S(1)}, bf16[1040,128]{1,0:T(8,128)(2,1)S(1)}, u32[]{:S(2)}, u32[]{:S(2)}) collective-permute-start(bf16[1040,128]{1,0:T(8,128)(2,1)S(1)} %collective-permute-done.1), channel_id=1, source_target_pairs={{0,2},{1,3},{2,0},{3,1},{4,5},{5,4},{6,7},{7,6},{8,10},{9,11},{10,... | collective-permute-start | bytes 798728 | tf_op jit(solution)/shard_map/ppermute | solution.py:333
  27.4 9.9 %collective-permute-start.10 = (bf16[1040,128]{1,0:T(8,128)(2,1)S(1)}, bf16[1040,128]{1,0:T(8,128)(2,1)S(1)}, u32[]{:S(2)}, u32[]{:S(2)}) collective-permute-start(bf16[1040,128]{1,0:T(8,128)(2,1)S(1)} %collective-permute-done.5), channel_id=1, source_target_pairs={{0,2},{1,3},{2,0},{3,1},{4,5},{5,4},{6,7},{7,6},{8,10},{9,11},{10,... | collective-permute-start | bytes 798728 | tf_op jit(solution)/shard_map/ppermute | solution.py:333
  28.0 11.9 %collective-permute-start.11 = (bf16[4160,128]{1,0:T(8,128)(2,1)S(1)}, bf16[4160,128]{1,0:T(8,128)(2,1)S(1)}, u32[]{:S(2)}, u32[]{:S(2)}) collective-permute-start(bf16[4160,128]{1,0:T(8,128)(2,1)S(1)} %pad_maximum_fusion.refs_0_), channel_id=1, source_target_pairs={{0,4},{1,5},{2,6},{3,7},{4,0},{5,1},{6,2},{7,3},{8,12},{9,13},{10,... | collective-permute-start | bytes 3194888 | tf_op jit(solution)/shard_map/ppermute | solution.py:333
  29.4 8.9 %collective-permute-start.2 = (bf16[1040,128]{1,0:T(8,128)(2,1)S(1)}, bf16[1040,128]{1,0:T(8,128)(2,1)S(1)}, u32[]{:S(2)}, u32[]{:S(2)}) collective-permute-start(bf16[1040,128]{1,0:T(8,128)(2,1)S(1)} %collective-permute-done.1), channel_id=1, source_target_pairs={{0,8},{1,9},{2,10},{3,11},{4,12},{5,13},{6,14},{7,15},{8,24},{9,25... | collective-permute-start | bytes 798728 | tf_op jit(solution)/shard_map/ppermute | solution.py:333
  37.4 17.2 %collective-permute-start.13 = (bf16[4160,128]{1,0:T(8,128)(2,1)S(1)}, bf16[4160,128]{1,0:T(8,128)(2,1)S(1)}, u32[]{:S(2)}, u32[]{:S(2)}) collective-permute-start(bf16[4160,128]{1,0:T(8,128)(2,1)S(1)} %constant_dynamic-update-slice_fusion.refs_0_), channel_id=1, source_target_pairs={{0,4},{1,5},{2,6},{3,7},{4,0},{5,1},{6,2},{7,3},{8,12},{9,13},{10,... | collective-permute-start | bytes 3194888 | tf_op jit(solution)/shard_map/ppermute | solution.py:333
  38.2 8.0 %collective-permute-start.17 = (bf16[1040,128]{1,0:T(8,128)(2,1)S(1)}, bf16[1040,128]{1,0:T(8,128)(2,1)S(1)}, u32[]{:S(2)}, u32[]{:S(2)}) collective-permute-start(bf16[1040,128]{1,0:T(8,128)(2,1)S(1)} %collective-permute-done.10), channel_id=1, source_target_pairs={{0,8},{1,9},{2,10},{3,11},{4,12},{5,13},{6,14},{7,15},{8,24},{9,25... | collective-permute-start | bytes 798728 | tf_op jit(solution)/shard_map/ppermute | solution.py:333
  42.8 5.8 %collective-permute-start.12 = (bf16[1040,128]{1,0:T(8,128)(2,1)S(1)}, bf16[1040,128]{1,0:T(8,128)(2,1)S(1)}, u32[]{:S(2)}, u32[]{:S(2)}) collective-permute-start(bf16[1040,128]{1,0:T(8,128)(2,1)S(1)} %collective-permute-done.2), channel_id=1, source_target_pairs={{0,1},{1,0},{2,3},{3,2},{4,6},{5,7},{6,4},{7,5},{8,9},{9,8},{10,11... | collective-permute-start | bytes 798728 | tf_op jit(solution)/shard_map/ppermute | solution.py:333
  46.2 12.6 %collective-permute-start.18 = (bf16[4160,128]{1,0:T(8,128)(2,1)S(1)}, bf16[4160,128]{1,0:T(8,128)(2,1)S(1)}, u32[]{:S(2)}, u32[]{:S(2)}) collective-permute-start(bf16[4160,128]{1,0:T(8,128)(2,1)S(1)} %constant_dynamic-update-slice_fusion.7.refs_0_), channel_id=1, source_target_pairs={{0,4},{1,5},{2,6},{3,7},{4,0},{5,1},{6,2},{7,3},{8,12},{9,13},{10,... | collective-permute-start | bytes 3194888 | tf_op jit(solution)/shard_map/ppermute | solution.py:333
  48.0 5.6 %collective-permute-start.15 = (bf16[1040,128]{1,0:T(8,128)(2,1)S(1)}, bf16[1040,128]{1,0:T(8,128)(2,1)S(1)}, u32[]{:S(2)}, u32[]{:S(2)}) collective-permute-start(bf16[1040,128]{1,0:T(8,128)(2,1)S(1)} %collective-permute-done.2), channel_id=1, source_target_pairs={{0,2},{1,3},{2,0},{3,1},{4,5},{5,4},{6,7},{7,6},{8,10},{9,11},{10,... | collective-permute-start | bytes 798728 | tf_op jit(solution)/shard_map/ppermute | solution.py:333
  53.6 8.9 %collective-permute-start.16 = (bf16[3120,128]{1,0:T(8,128)(2,1)S(1)}, bf16[3120,128]{1,0:T(8,128)(2,1)S(1)}, u32[]{:S(2)}, u32[]{:S(2)}) collective-permute-start(bf16[3120,128]{1,0:T(8,128)(2,1)S(1)} %constant_dynamic-update-slice_fusion.4.refs_0_), channel_id=1, source_target_pairs={{0,4},{1,5},{2,6},{3,7},{4,0},{5,1},{6,2},{7,3},{8,12},{9,13},{10,... | collective-permute-start | bytes 2396168 | tf_op jit(solution)/shard_map/ppermute | solution.py:333
  58.1 7.2 %collective-permute-start.14 = (bf16[1040,128]{1,0:T(8,128)(2,1)S(1)}, bf16[1040,128]{1,0:T(8,128)(2,1)S(1)}, u32[]{:S(2)}, u32[]{:S(2)}) collective-permute-start(bf16[1040,128]{1,0:T(8,128)(2,1)S(1)} %collective-permute-done.12), channel_id=1, source_target_pairs={{0,2},{1,3},{2,0},{3,1},{4,5},{5,4},{6,7},{7,6},{8,10},{9,11},{10,... | collective-permute-start | bytes 798728 | tf_op jit(solution)/shard_map/ppermute | solution.py:333
  65.3 1.6 %collective-permute-start.19 = (bf16[1040,128]{1,0:T(8,128)(2,1)S(1)}, bf16[1040,128]{1,0:T(8,128)(2,1)S(1)}, u32[]{:S(2)}, u32[]{:S(2)}) collective-permute-start(bf16[1040,128]{1,0:T(8,128)(2,1)S(1)} %collective-permute-done.14.refs_0_), channel_id=1, source_target_pairs={{0,4},{1,5},{2,6},{3,7},{4,0},{5,1},{6,2},{7,3},{8,12},{9,13},{10,... | collective-permute-start | bytes 798728 | tf_op jit(solution)/shard_map/ppermute | solution.py:333

commit v2 on v1

--- a/solution.py
+++ b/solution.py
@@ -282,7 +282,7 @@
             compiler_params=pltpu.CompilerParams(vmem_limit_bytes=28 * 1024 * 1024),
             cost_estimate=pl.CostEstimate(
                 flops=count * RUN * self.q.size * 4,
-                bytes_accessed=self.q.size * 8,
+                bytes_accessed=self.q.size * count,
                 transcendentals=0,
             ),
             name=name,
@@ -292,7 +292,7 @@
         kernel = functools.partial(own_kernel, self.group, self.factor, self.half)
         return self.call(kernel, [self.q, own], self.carried, {}, 2, "attend_own")
 
-    def add(self, state, kvs, keep=KEEP, out=None):
+    def add(self, state, kvs, keep=KEEP, weight=1, out=None):
         kvs = [x if isinstance(x, tuple) else (x, 0) for x in kvs]
         blocks = [(skip, x.shape[0] // self.block_rows) for x, skip in kvs]
         count = sum(end - skip for skip, end in blocks)
@@ -302,7 +302,7 @@
         kernel = functools.partial(
             attend_kernel, self.group, self.factor, self.half, ahead, keep, blocks
         )
-        results = self.call(kernel, operands, self.carried, aliases, count, "attend", out)
+        results = self.call(kernel, operands, self.carried, aliases, count * weight, "attend", out)
         return results[0] if ahead else results
 
 
@@ -379,7 +379,7 @@
     stages = [own]
     for n in range(1, chips):
         stages.append(along_z(stages[-1]))
-    planes, ready = [], []
+    planes, waiting, late = [], None, []
     for n in range(chips):
         stage = stages[n]
         before = planes[n - 1] if n else {}
@@ -387,18 +387,13 @@
             earlier = [before[m] for m in single]
             if n > 1:
                 earlier += [planes[n - 2][m] for m in several]
-            if n > 2:
-                state = attention.add(state, ready[n - 3])
-                earlier.append(state[0])
             stage = tied(stage, *earlier)
         found = {0: stage}
         for step in range(bits):
             found[1 << step] = over_place(stage, step)
-        if n + 1 < chips:
-            wait_for = [stages[n + 1]] + ([state[0]] if n == 0 else [])
-        else:
-            state = attention.add(state, ready[n - 2])
-            wait_for = [state[0]]
+        wait_for = stages[n + 1 : n + 2]
+        if n == 0:
+            wait_for.append(state[0])
         for m in several:
             if n + 2 == chips:
                 found[m] = along_z(tied(before[m], *wait_for))
@@ -406,18 +401,21 @@
                 top = m.bit_length() - 1
                 found[m] = over_place(tied(found[m - (1 << top)], *wait_for), top)
         planes.append(found)
-        if n + 1 < chips:
-            held = jnp.concatenate([found[m] for m in range(inner)])
-            ready.append([(held, int(n == 0)), other_core(held)])
-    waiting = ready[-1]
-    *most, final = (found[m] for m in range(inner))
-    most = jnp.concatenate(most)
-    theirs = other_core(most)
-    state = attention.add(state, waiting)
-    state = attention.add(state, [most, theirs])
-    final = tied(final, state[0])
-    theirs = other_core(final)
-    state = attention.add(state, [final], keep=1)
+        now = [found[m] for m in range(inner) if not (n + 2 >= chips and m in several)]
+        if n + 2 >= chips:
+            late += [found[m] for m in several]
+        held = jnp.concatenate(now)
+        if waiting:
+            weight = 3 if n + 1 == chips else 3 if n + 2 == chips else 1
+            state = attention.add(state, waiting, weight=weight)
+            if n + 1 < chips:
+                held = tied(held, state[0])
+        waiting = [(held, int(n == 0)), other_core(held)]
+
+    state = attention.add(state, waiting, weight=3)
+    held = jnp.concatenate([tied(x, state[0]) for x in late])
+    theirs = other_core(held)
+    state = attention.add(state, [held], keep=1)
     out = jax.ShapeDtypeStruct(queries.shape, queries.dtype)
     return attention.add(state, [theirs], keep=1, out=out)
 

time: 70.8 us -> 67.5 us (0.953)
  waiting for transfers between devices: 26.9 us -> 11.4 us
  starting transfers between devices: 20.7 us -> 34.1 us
  Pallas kernels: 19.8 us -> 18.8 us
    ppermute x20, waiting for transfers between devices: 26.9 us -> 11.4 us  [permute(): return lax.ppermute(x, AXES, pairs)]
    ppermute x20, starting transfers between devices: 20.7 us -> 34.1 us  [permute(): return lax.ppermute(x, AXES, pairs)]
    pallas_call x7, Pallas kernels: 17.7 us -> 16.7 us  [call(): pl.pallas_call(kernel, out_shape=shapes, in_specs=[vmem] * len(operands),...]
  transfers between devices with their start and end apart: 20 -> 20, of which waited for: 9 -> 8; matrix products, arithmetic and copies ran while one was open for 3% -> 3% of each run, Pallas kernels for 22% -> 23%
where the time goes in v2:
time: 67.5 us; the launch traced here: 66.4 us
  starting transfers between devices  34.1 us (51%)
  Pallas kernels  18.8 us (28%)
  waiting for transfers between devices  11.4 us (17%)
  local copies, waits for them, and re-layouts  1.56 us (2%)
    ppermute x20, starting transfers between devices, permute(): return lax.ppermute(x, AXES, pairs)  34.1 us
    pallas_call x7, Pallas kernels, call(): pl.pallas_call(kernel, out_shape=shapes, in_specs=[vmem] * len(operands),...  16.7 us
    ppermute x20, waiting for transfers between devices, permute(): return lax.ppermute(x, AXES, pairs)  11.4 us
    pallas_call x1, Pallas kernels, per_device(): pl.pallas_call(pack_kernel, out_shape=jax.ShapeDtypeStruct((2 * tokens *...  2.08 us
    reshape x1, local copies, waits for them, and re-layouts, per_device(): queries.reshape(2, RUN, heads_kv, group, head_dim).transpose(0, 2, 1, 3, 4)  1.41 us
  transfers between devices with their start and end apart: 20, of which 8 were waited for; matrix products, arithmetic and copies ran while one was open for 3% of the time, Pallas kernels for 23%

profile of v2, /device:TPU:1, one launch (start us, length us, event | category | flops | bytes accessed | tf_op | source)
XLA Modules:
  0.0 66.4 jit_solution(9996168184737327223)
XLA Ops:
  0.0 2.1 %pack.1.own_ref = bf16[1040,128]{1,0:T(8,128)(2,1)} custom-call(bf16[512,128]{1,0:T(8,128)(2,1)} %bitcast.17, bf16[512,128]{1,0:T(8,128)(2,1)} %bitcast.18, s32[1,128]{1,0:T(1,128)} %bitcast.19), custom_call_target="tpu_custom_call" | custom-call | tf_op jit(solution)/shard_map/pack/pallas_call | solution.py:351
  2.1 0.0 copy-start
  2.1 2.2 %collective-permute-start = (bf16[1040,128]{1,0:T(8,128)(2,1)}, bf16[1040,128]{1,0:T(8,128)(2,1)S(1)}, u32[]{:S(2)}, u32[]{:S(2)}) collective-permute-start(bf16[1040,128]{1,0:T(8,128)(2,1)} %pack.1.own_ref), channel_id=1, source_target_pairs={{0,8},{1,9},{2,10},{3,11},{4,12},{5,13},{6,14},{7,15},{8,24},{9,25... | collective-permute-start | bytes 798728 | tf_op jit(solution)/shard_map/ppermute | solution.py:333
  4.3 1.2 %collective-permute-start.1 = (bf16[1040,128]{1,0:T(8,128)(2,1)}, bf16[1040,128]{1,0:T(8,128)(2,1)S(1)}, u32[]{:S(2)}, u32[]{:S(2)}) collective-permute-start(bf16[1040,128]{1,0:T(8,128)(2,1)} %pack.1.own_ref), channel_id=1, source_target_pairs={{0,1},{1,0},{2,3},{3,2},{4,6},{5,7},{6,4},{7,5},{8,9},{9,8},{10,11... | collective-permute-start | bytes 798728 | tf_op jit(solution)/shard_map/ppermute | solution.py:333
  5.5 1.2 %collective-permute-start.2 = (bf16[1040,128]{1,0:T(8,128)(2,1)}, bf16[1040,128]{1,0:T(8,128)(2,1)S(1)}, u32[]{:S(2)}, u32[]{:S(2)}) collective-permute-start(bf16[1040,128]{1,0:T(8,128)(2,1)} %pack.1.own_ref), channel_id=1, source_target_pairs={{0,2},{1,3},{2,0},{3,1},{4,5},{5,4},{6,7},{7,6},{8,10},{9,11},{10,... | collective-permute-start | bytes 798728 | tf_op jit(solution)/shard_map/ppermute | solution.py:333
  6.7 1.4 %copy.37 = bf16[2,64,4,8,128]{4,3,1,2,0:T(8,128)(2,1)S(1)} copy(bf16[2,64,4,8,128]{4,3,2,1,0:T(8,128)(2,1)} %bitcast.16) | data formatting | bytes 2097152 | tf_op jit(solution)/shard_map/reshape | solution.py:368
  8.2 1.2 %attend_own.1 = (f32[8,128]{1,0:T(8,128)S(1)}, f32[2,4,512,128]{3,2,1,0:T(8,128)S(1)}, f32[2,4,512,128]{3,2,1,0:T(8,128)S(1)}, f32[2,4,512,128]{3,2,1,0:T(8,128)S(1)}, bf16[2,20,512,128]{3,2,1,0:T(8,128)(2,1)S(1)}) custom-call(bf16[2,4,512,128]{3,2,1,0:T(8,128)(2,1)S(1)} %bitcast.9, bf16[1040,128]{1,0:T(8,128)(2,1)S(1)} %copy-done), custom_call_target="tpu_custom_call" | custom-call | flops 268435456 | bytes 1048576 | tf_op jit(solution)/shard_map/attend_own/pallas_call | solution.py:275
  9.3 2.3 %collective-permute-done = bf16[1040,128]{1,0:T(8,128)(2,1)S(1)} collective-permute-done((bf16[1040,128]{1,0:T(8,128)(2,1)}, bf16[1040,128]{1,0:T(8,128)(2,1)S(1)}, u32[]{:S(2)}, u32[]{:S(2)}) %collective-permute-start) | collective-permute-done | bytes 266272 | tf_op jit(solution)/shard_map/ppermute | solution.py:333
  11.6 0.0 collective-permute-done.1
  11.6 0.9 %collective-permute-start.9 = (bf16[1040,128]{1,0:T(8,128)(2,1)S(1)}, bf16[1040,128]{1,0:T(8,128)(2,1)S(1)}, u32[]{:S(2)}, u32[]{:S(2)}) collective-permute-start(bf16[1040,128]{1,0:T(8,128)(2,1)S(1)} %collective-permute-done.1), channel_id=1, source_target_pairs={{0,2},{1,3},{2,0},{3,1},{4,5},{5,4},{6,7},{7,6},{8,10},{9,11},{10,... | collective-permute-start | bytes 798728 | tf_op jit(solution)/shard_map/ppermute | solution.py:333
  12.6 1.4 %collective-permute-done.2 = bf16[1040,128]{1,0:T(8,128)(2,1)S(1)} collective-permute-done((bf16[1040,128]{1,0:T(8,128)(2,1)}, bf16[1040,128]{1,0:T(8,128)(2,1)S(1)}, u32[]{:S(2)}, u32[]{:S(2)}) %collective-permute-start.2) | collective-permute-done | bytes 266272 | tf_op jit(solution)/shard_map/ppermute | solution.py:333
  14.0 0.0 collective-permute-start.3
  14.0 2.3 %collective-permute-start.4 = (bf16[1040,128]{1,0:T(8,128)(2,1)S(1)}, bf16[1040,128]{1,0:T(8,128)(2,1)S(1)}, u32[]{:S(2)}, u32[]{:S(2)}) collective-permute-start(bf16[1040,128]{1,0:T(8,128)(2,1)S(1)} %collective-permute-done), channel_id=1, source_target_pairs={{0,8},{1,9},{2,10},{3,11},{4,12},{5,13},{6,14},{7,15},{8,24},{9,25... | collective-permute-start | bytes 798728 | tf_op jit(solution)/shard_map/ppermute | solution.py:333
  16.3 0.6 collective-permute-done.9
  16.9 0.1 pad_maximum_fusion.1.refs_0_
  17.0 5.9 %collective-permute-start.15 = (bf16[4160,128]{1,0:T(8,128)(2,1)S(1)}, bf16[4160,128]{1,0:T(8,128)(2,1)S(1)}, u32[]{:S(2)}, u32[]{:S(2)}) collective-permute-start(bf16[4160,128]{1,0:T(8,128)(2,1)S(1)} %pad_maximum_fusion.1.refs_0_), channel_id=1, source_target_pairs={{0,4},{1,5},{2,6},{3,7},{4,0},{5,1},{6,2},{7,3},{8,12},{9,13},{10,... | collective-permute-start | bytes 3194888 | tf_op jit(solution)/shard_map/ppermute | solution.py:333
  22.9 1.2 %collective-permute-start.8 = (bf16[1040,128]{1,0:T(8,128)(2,1)S(1)}, bf16[1040,128]{1,0:T(8,128)(2,1)S(1)}, u32[]{:S(2)}, u32[]{:S(2)}) collective-permute-start(bf16[1040,128]{1,0:T(8,128)(2,1)S(1)} %collective-permute-done), channel_id=1, source_target_pairs={{0,2},{1,3},{2,0},{3,1},{4,5},{5,4},{6,7},{7,6},{8,10},{9,11},{10,... | collective-permute-start | bytes 798728 | tf_op jit(solution)/shard_map/ppermute | solution.py:333
  24.1 0.3 collective-permute-start.5
  24.4 4.1 %collective-permute-done.8 = bf16[1040,128]{1,0:T(8,128)(2,1)S(1)} collective-permute-done((bf16[1040,128]{1,0:T(8,128)(2,1)S(1)}, bf16[1040,128]{1,0:T(8,128)(2,1)S(1)}, u32[]{:S(2)}, u32[]{:S(2)}) %collective-permute-start.8) | collective-permute-done | bytes 266272 | tf_op jit(solution)/shard_map/ppermute | solution.py:333
  28.5 0.0 collective-permute-start.10
  28.5 1.2 %collective-permute-start.11 = (bf16[1040,128]{1,0:T(8,128)(2,1)S(1)}, bf16[1040,128]{1,0:T(8,128)(2,1)S(1)}, u32[]{:S(2)}, u32[]{:S(2)}) collective-permute-start(bf16[1040,128]{1,0:T(8,128)(2,1)S(1)} %collective-permute-done.4), channel_id=1, source_target_pairs={{0,2},{1,3},{2,0},{3,1},{4,5},{5,4},{6,7},{7,6},{8,10},{9,11},{10,... | collective-permute-start | bytes 798728 | tf_op jit(solution)/shard_map/ppermute | solution.py:333
  29.7 2.3 %collective-permute-start.6 = (bf16[1040,128]{1,0:T(8,128)(2,1)S(1)}, bf16[1040,128]{1,0:T(8,128)(2,1)S(1)}, u32[]{:S(2)}, u32[]{:S(2)}) collective-permute-start(bf16[1040,128]{1,0:T(8,128)(2,1)S(1)} %collective-permute-done.4), channel_id=1, source_target_pairs={{0,8},{1,9},{2,10},{3,11},{4,12},{5,13},{6,14},{7,15},{8,24},{9,25... | collective-permute-start | bytes 798728 | tf_op jit(solution)/shard_map/ppermute | solution.py:333
  32.0 0.0 collective-permute-done.5
  32.0 0.1 pad_maximum_fusion.refs_0_
  32.1 0.0 collective-permute-done.15.refs_1_
  32.1 1.8 %attend.6 = (f32[8,128]{1,0:T(8,128)S(1)}, f32[2,4,512,128]{3,2,1,0:T(8,128)S(1)}, f32[2,4,512,128]{3,2,1,0:T(8,128)S(1)}, f32[2,4,512,128]{3,2,1,0:T(8,128)S(1)}, bf16[2,20,512,128]{3,2,1,0:T(8,128)(2,1)S(1)}) custom-call(bf16[2,4,512,128]{3,2,1,0:T(8,128)(2,1)S(1)} %bitcast.10, ...), custom_call_target="tpu_custom_call", output_to_operand_aliasing={{0}: (3, {}), {1}: (4, {}), {2}: (5, {}), {3}: (6, {}), {4}... | custom-call | flops 939524096 | bytes 3670016 | tf_op jit(solution)/shard_map/attend/pallas_call | solution.py:275
  33.9 3.0 %collective-permute-start.16 = (bf16[4160,128]{1,0:T(8,128)(2,1)S(1)}, bf16[4160,128]{1,0:T(8,128)(2,1)S(1)}, u32[]{:S(2)}, u32[]{:S(2)}) collective-permute-start(bf16[4160,128]{1,0:T(8,128)(2,1)S(1)} %pad_maximum_fusion.refs_0_), channel_id=1, source_target_pairs={{0,4},{1,5},{2,6},{3,7},{4,0},{5,1},{6,2},{7,3},{8,12},{9,13},{10,... | collective-permute-start | bytes 3194888 | tf_op jit(solution)/shard_map/ppermute | solution.py:333
  36.9 0.0 collective-permute-done.10
  36.9 0.1 collective-permute-done.6
  37.0 1.5 %collective-permute-start.12 = (bf16[1040,128]{1,0:T(8,128)(2,1)S(1)}, bf16[1040,128]{1,0:T(8,128)(2,1)S(1)}, u32[]{:S(2)}, u32[]{:S(2)}) collective-permute-start(bf16[1040,128]{1,0:T(8,128)(2,1)S(1)} %collective-permute-done.6), channel_id=1, source_target_pairs={{0,1},{1,0},{2,3},{3,2},{4,6},{5,7},{6,4},{7,5},{8,9},{9,8},{10,11... | collective-permute-start | bytes 798728 | tf_op jit(solution)/shard_map/ppermute | solution.py:333
  38.4 1.1 %collective-permute-start.13 = (bf16[1040,128]{1,0:T(8,128)(2,1)S(1)}, bf16[1040,128]{1,0:T(8,128)(2,1)S(1)}, u32[]{:S(2)}, u32[]{:S(2)}) collective-permute-start(bf16[1040,128]{1,0:T(8,128)(2,1)S(1)} %collective-permute-done.6), channel_id=1, source_target_pairs={{0,2},{1,3},{2,0},{3,1},{4,5},{5,4},{6,7},{7,6},{8,10},{9,11},{10,... | collective-permute-start | bytes 798728 | tf_op jit(solution)/shard_map/ppermute | solution.py:333
  39.5 0.1 pad_maximum_fusion.2.refs_0_
  39.6 2.7 %collective-permute-done.12 = bf16[1040,128]{1,0:T(8,128)(2,1)S(1)} collective-permute-done((bf16[1040,128]{1,0:T(8,128)(2,1)S(1)}, bf16[1040,128]{1,0:T(8,128)(2,1)S(1)}, u32[]{:S(2)}, u32[]{:S(2)}) %collective-permute-start.12) | collective-permute-done | bytes 266272 | tf_op jit(solution)/shard_map/ppermute | solution.py:333
  42.3 3.0 %attend.7 = (f32[8,128]{1,0:T(8,128)S(1)}, f32[2,4,512,128]{3,2,1,0:T(8,128)S(1)}, f32[2,4,512,128]{3,2,1,0:T(8,128)S(1)}, f32[2,4,512,128]{3,2,1,0:T(8,128)S(1)}, bf16[2,20,512,128]{3,2,1,0:T(8,128)(2,1)S(1)}) custom-call(bf16[2,4,512,128]{3,2,1,0:T(8,128)(2,1)S(1)} %bitcast.11, ...), custom_call_target="tpu_custom_call", output_to_operand_aliasing={{0}: (3, {}), {1}: (4, {}), {2}: (5, {}), {3}: (6, {}), {4}... | custom-call | flops 3221225472 | bytes 12582912 | tf_op jit(solution)/shard_map/attend/pallas_call | solution.py:275
  45.3 5.1 %collective-permute-start.17 = (bf16[3120,128]{1,0:T(8,128)(2,1)S(1)}, bf16[3120,128]{1,0:T(8,128)(2,1)S(1)}, u32[]{:S(2)}, u32[]{:S(2)}) collective-permute-start(bf16[3120,128]{1,0:T(8,128)(2,1)S(1)} %pad_maximum_fusion.2.refs_0_), channel_id=1, source_target_pairs={{0,4},{1,5},{2,6},{3,7},{4,0},{5,1},{6,2},{7,3},{8,12},{9,13},{10,... | collective-permute-start | bytes 2396168 | tf_op jit(solution)/shard_map/ppermute | solution.py:333
  50.4 0.1 collective-permute-start.14
  50.5 2.8 %collective-permute-start.7 = (bf16[1040,128]{1,0:T(8,128)(2,1)S(1)}, bf16[1040,128]{1,0:T(8,128)(2,1)S(1)}, u32[]{:S(2)}, u32[]{:S(2)}) collective-permute-start(bf16[1040,128]{1,0:T(8,128)(2,1)S(1)} %collective-permute-done.5), channel_id=1, source_target_pairs={{0,8},{1,9},{2,10},{3,11},{4,12},{5,13},{6,14},{7,15},{8,24},{9,25... | collective-permute-start | bytes 798728 | tf_op jit(solution)/shard_map/ppermute | solution.py:333
  53.2 0.1 collective-permute-start.18
  53.3 0.0 collective-permute-done.17.refs_1_
  53.3 3.7 %attend.8 = (f32[8,128]{1,0:T(8,128)S(1)}, f32[2,4,512,128]{3,2,1,0:T(8,128)S(1)}, f32[2,4,512,128]{3,2,1,0:T(8,128)S(1)}, f32[2,4,512,128]{3,2,1,0:T(8,128)S(1)}, bf16[2,20,512,128]{3,2,1,0:T(8,128)(2,1)S(1)}) custom-call(bf16[2,4,512,128]{3,2,1,0:T(8,128)(2,1)S(1)} %bitcast.12, ...), custom_call_target="tpu_custom_call", output_to_operand_aliasing={{0}: (3, {}), {1}: (4, {}), {2}: (5, {}), {3}: (6, {}), {4}... | custom-call | flops 2415919104 | bytes 9437184 | tf_op jit(solution)/shard_map/attend/pallas_call | solution.py:275
  57.0 0.0 collective-permute-done.14.refs_1_
  57.0 1.7 %attend.9 = (f32[8,128]{1,0:T(8,128)S(1)}, f32[2,4,512,128]{3,2,1,0:T(8,128)S(1)}, f32[2,4,512,128]{3,2,1,0:T(8,128)S(1)}, f32[2,4,512,128]{3,2,1,0:T(8,128)S(1)}, bf16[2,20,512,128]{3,2,1,0:T(8,128)(2,1)S(1)}) custom-call(bf16[2,4,512,128]{3,2,1,0:T(8,128)(2,1)S(1)} %bitcast.13, ...), custom_call_target="tpu_custom_call", output_to_operand_aliasing={{0}: (3, {}), {1}: (4, {}), {2}: (5, {}), {3}: (6, {}), {4}... | custom-call | flops 2415919104 | bytes 9437184 | tf_op jit(solution)/shard_map/attend/pallas_call | solution.py:275
  58.7 0.1 collective-permute-done.18
  58.8 0.1 collective-permute-done.7
  59.0 1.8 %collective-permute-start.19 = (bf16[2080,128]{1,0:T(8,128)(2,1)S(1)}, bf16[2080,128]{1,0:T(8,128)(2,1)S(1)}, u32[]{:S(2)}, u32[]{:S(2)}) collective-permute-start(bf16[2080,128]{1,0:T(8,128)(2,1)S(1)} %constant_dynamic-update-slice_fusion.3.refs_0_), channel_id=1, source_target_pairs={{0,4},{1,5},{2,6},{3,7},{4,0},{5,1},{6,2},{7,3},{8,12},{9,13},{10,... | collective-permute-start | bytes 1597448 | tf_op jit(solution)/shard_map/ppermute | solution.py:333
  60.8 3.8 %attend.10 = (f32[8,128]{1,0:T(8,128)S(1)}, f32[2,4,512,128]{3,2,1,0:T(8,128)S(1)}, f32[2,4,512,128]{3,2,1,0:T(8,128)S(1)}, f32[2,4,512,128]{3,2,1,0:T(8,128)S(1)}, bf16[2,20,512,128]{3,2,1,0:T(8,128)(2,1)S(1)}) custom-call(bf16[2,4,512,128]{3,2,1,0:T(8,128)(2,1)S(1)} %bitcast.14, ...), custom_call_target="tpu_custom_call", output_to_operand_aliasing={{0}: (2, {}), {1}: (3, {}), {2}: (4, {}), {3}: (5, {}), {4}... | custom-call | flops 268435456 | bytes 1048576 | tf_op jit(solution)/shard_map/attend/pallas_call | solution.py:275
  64.6 0.0 collective-permute-done.19.refs_0_
  64.6 1.7 %attend.11 = (bf16[128,32,128]{2,1,0:T(8,128)(2,1)}, f32[8,128]{1,0:T(8,128)S(1)}, f32[2,4,512,128]{3,2,1,0:T(8,128)S(1)}, f32[2,4,512,128]{3,2,1,0:T(8,128)S(1)...) custom-call(bf16[2,4,512,128]{3,2,1,0:T(8,128)(2,1)S(1)} %bitcast.15, ...), custom_call_target="tpu_custom_call", output_to_operand_aliasing={{1}: (2, {}), {2}: (3, {}), {3}: (4, {}), {4}: (5, {}), {5}... | custom-call | flops 268435456 | bytes 1048576 | tf_op jit(solution)/shard_map/attend/pallas_call | solution.py:275
  (11 shorter events, 0.2 us)
Async XLA Ops:
  2.1 6.1 %copy-start = (bf16[1040,128]{1,0:T(8,128)(2,1)S(1)}, bf16[1040,128]{1,0:T(8,128)(2,1)}, u32[]{:S(2)}) copy-start(bf16[1040,128]{1,0:T(8,128)(2,1)} %pack.1.own_ref) | copy-start | bytes 798724
  2.1 9.5 %collective-permute-start = (bf16[1040,128]{1,0:T(8,128)(2,1)}, bf16[1040,128]{1,0:T(8,128)(2,1)S(1)}, u32[]{:S(2)}, u32[]{:S(2)}) collective-permute-start(bf16[1040,128]{1,0:T(8,128)(2,1)} %pack.1.own_ref), channel_id=1, source_target_pairs={{0,8},{1,9},{2,10},{3,11},{4,12},{5,13},{6,14},{7,15},{8,24},{9,25... | collective-permute-start | bytes 798728 | tf_op jit(solution)/shard_map/ppermute | solution.py:333
  4.3 7.4 %collective-permute-start.1 = (bf16[1040,128]{1,0:T(8,128)(2,1)}, bf16[1040,128]{1,0:T(8,128)(2,1)S(1)}, u32[]{:S(2)}, u32[]{:S(2)}) collective-permute-start(bf16[1040,128]{1,0:T(8,128)(2,1)} %pack.1.own_ref), channel_id=1, source_target_pairs={{0,1},{1,0},{2,3},{3,2},{4,6},{5,7},{6,4},{7,5},{8,9},{9,8},{10,11... | collective-permute-start | bytes 798728 | tf_op jit(solution)/shard_map/ppermute | solution.py:333
  5.5 8.4 %collective-permute-start.2 = (bf16[1040,128]{1,0:T(8,128)(2,1)}, bf16[1040,128]{1,0:T(8,128)(2,1)S(1)}, u32[]{:S(2)}, u32[]{:S(2)}) collective-permute-start(bf16[1040,128]{1,0:T(8,128)(2,1)} %pack.1.own_ref), channel_id=1, source_target_pairs={{0,2},{1,3},{2,0},{3,1},{4,5},{5,4},{6,7},{7,6},{8,10},{9,11},{10,... | collective-permute-start | bytes 798728 | tf_op jit(solution)/shard_map/ppermute | solution.py:333
  11.6 5.3 %collective-permute-start.9 = (bf16[1040,128]{1,0:T(8,128)(2,1)S(1)}, bf16[1040,128]{1,0:T(8,128)(2,1)S(1)}, u32[]{:S(2)}, u32[]{:S(2)}) collective-permute-start(bf16[1040,128]{1,0:T(8,128)(2,1)S(1)} %collective-permute-done.1), channel_id=1, source_target_pairs={{0,2},{1,3},{2,0},{3,1},{4,5},{5,4},{6,7},{7,6},{8,10},{9,11},{10,... | collective-permute-start | bytes 798728 | tf_op jit(solution)/shard_map/ppermute | solution.py:333
  14.0 10.2 %collective-permute-start.3 = (bf16[1040,128]{1,0:T(8,128)(2,1)S(1)}, bf16[1040,128]{1,0:T(8,128)(2,1)S(1)}, u32[]{:S(2)}, u32[]{:S(2)}) collective-permute-start(bf16[1040,128]{1,0:T(8,128)(2,1)S(1)} %collective-permute-done), channel_id=1, source_target_pairs={{0,1},{1,0},{2,3},{3,2},{4,6},{5,7},{6,4},{7,5},{8,9},{9,8},{10,11... | collective-permute-start | bytes 798728 | tf_op jit(solution)/shard_map/ppermute | solution.py:333
  14.0 10.2 %collective-permute-start.4 = (bf16[1040,128]{1,0:T(8,128)(2,1)S(1)}, bf16[1040,128]{1,0:T(8,128)(2,1)S(1)}, u32[]{:S(2)}, u32[]{:S(2)}) collective-permute-start(bf16[1040,128]{1,0:T(8,128)(2,1)S(1)} %collective-permute-done), channel_id=1, source_target_pairs={{0,8},{1,9},{2,10},{3,11},{4,12},{5,13},{6,14},{7,15},{8,24},{9,25... | collective-permute-start | bytes 798728 | tf_op jit(solution)/shard_map/ppermute | solution.py:333
  17.0 15.1 %collective-permute-start.15 = (bf16[4160,128]{1,0:T(8,128)(2,1)S(1)}, bf16[4160,128]{1,0:T(8,128)(2,1)S(1)}, u32[]{:S(2)}, u32[]{:S(2)}) collective-permute-start(bf16[4160,128]{1,0:T(8,128)(2,1)S(1)} %pad_maximum_fusion.1.refs_0_), channel_id=1, source_target_pairs={{0,4},{1,5},{2,6},{3,7},{4,0},{5,1},{6,2},{7,3},{8,12},{9,13},{10,... | collective-permute-start | bytes 3194888 | tf_op jit(solution)/shard_map/ppermute | solution.py:333
  22.9 5.6 %collective-permute-start.8 = (bf16[1040,128]{1,0:T(8,128)(2,1)S(1)}, bf16[1040,128]{1,0:T(8,128)(2,1)S(1)}, u32[]{:S(2)}, u32[]{:S(2)}) collective-permute-start(bf16[1040,128]{1,0:T(8,128)(2,1)S(1)} %collective-permute-done), channel_id=1, source_target_pairs={{0,2},{1,3},{2,0},{3,1},{4,5},{5,4},{6,7},{7,6},{8,10},{9,11},{10,... | collective-permute-start | bytes 798728 | tf_op jit(solution)/shard_map/ppermute | solution.py:333
  24.1 7.9 %collective-permute-start.5 = (bf16[1040,128]{1,0:T(8,128)(2,1)S(1)}, bf16[1040,128]{1,0:T(8,128)(2,1)S(1)}, u32[]{:S(2)}, u32[]{:S(2)}) collective-permute-start(bf16[1040,128]{1,0:T(8,128)(2,1)S(1)} %collective-permute-done.3), channel_id=1, source_target_pairs={{0,2},{1,3},{2,0},{3,1},{4,5},{5,4},{6,7},{7,6},{8,10},{9,11},{10,... | collective-permute-start | bytes 798728 | tf_op jit(solution)/shard_map/ppermute | solution.py:333
  28.5 8.4 %collective-permute-start.10 = (bf16[1040,128]{1,0:T(8,128)(2,1)S(1)}, bf16[1040,128]{1,0:T(8,128)(2,1)S(1)}, u32[]{:S(2)}, u32[]{:S(2)}) collective-permute-start(bf16[1040,128]{1,0:T(8,128)(2,1)S(1)} %collective-permute-done.4), channel_id=1, source_target_pairs={{0,1},{1,0},{2,3},{3,2},{4,6},{5,7},{6,4},{7,5},{8,9},{9,8},{10,11... | collective-permute-start | bytes 798728 | tf_op jit(solution)/shard_map/ppermute | solution.py:333
  28.5 8.4 %collective-permute-start.11 = (bf16[1040,128]{1,0:T(8,128)(2,1)S(1)}, bf16[1040,128]{1,0:T(8,128)(2,1)S(1)}, u32[]{:S(2)}, u32[]{:S(2)}) collective-permute-start(bf16[1040,128]{1,0:T(8,128)(2,1)S(1)} %collective-permute-done.4), channel_id=1, source_target_pairs={{0,2},{1,3},{2,0},{3,1},{4,5},{5,4},{6,7},{7,6},{8,10},{9,11},{10,... | collective-permute-start | bytes 798728 | tf_op jit(solution)/shard_map/ppermute | solution.py:333
  29.7 7.3 %collective-permute-start.6 = (bf16[1040,128]{1,0:T(8,128)(2,1)S(1)}, bf16[1040,128]{1,0:T(8,128)(2,1)S(1)}, u32[]{:S(2)}, u32[]{:S(2)}) collective-permute-start(bf16[1040,128]{1,0:T(8,128)(2,1)S(1)} %collective-permute-done.4), channel_id=1, source_target_pairs={{0,8},{1,9},{2,10},{3,11},{4,12},{5,13},{6,14},{7,15},{8,24},{9,25... | collective-permute-start | bytes 798728 | tf_op jit(solution)/shard_map/ppermute | solution.py:333
  33.9 8.4 %collective-permute-start.16 = (bf16[4160,128]{1,0:T(8,128)(2,1)S(1)}, bf16[4160,128]{1,0:T(8,128)(2,1)S(1)}, u32[]{:S(2)}, u32[]{:S(2)}) collective-permute-start(bf16[4160,128]{1,0:T(8,128)(2,1)S(1)} %pad_maximum_fusion.refs_0_), channel_id=1, source_target_pairs={{0,4},{1,5},{2,6},{3,7},{4,0},{5,1},{6,2},{7,3},{8,12},{9,13},{10,... | collective-permute-start | bytes 3194888 | tf_op jit(solution)/shard_map/ppermute | solution.py:333
  37.0 5.3 %collective-permute-start.12 = (bf16[1040,128]{1,0:T(8,128)(2,1)S(1)}, bf16[1040,128]{1,0:T(8,128)(2,1)S(1)}, u32[]{:S(2)}, u32[]{:S(2)}) collective-permute-start(bf16[1040,128]{1,0:T(8,128)(2,1)S(1)} %collective-permute-done.6), channel_id=1, source_target_pairs={{0,1},{1,0},{2,3},{3,2},{4,6},{5,7},{6,4},{7,5},{8,9},{9,8},{10,11... | collective-permute-start | bytes 798728 | tf_op jit(solution)/shard_map/ppermute | solution.py:333
  38.4 11.9 %collective-permute-start.13 = (bf16[1040,128]{1,0:T(8,128)(2,1)S(1)}, bf16[1040,128]{1,0:T(8,128)(2,1)S(1)}, u32[]{:S(2)}, u32[]{:S(2)}) collective-permute-start(bf16[1040,128]{1,0:T(8,128)(2,1)S(1)} %collective-permute-done.6), channel_id=1, source_target_pairs={{0,2},{1,3},{2,0},{3,1},{4,5},{5,4},{6,7},{7,6},{8,10},{9,11},{10,... | collective-permute-start | bytes 798728 | tf_op jit(solution)/shard_map/ppermute | solution.py:333
  45.3 8.1 %collective-permute-start.17 = (bf16[3120,128]{1,0:T(8,128)(2,1)S(1)}, bf16[3120,128]{1,0:T(8,128)(2,1)S(1)}, u32[]{:S(2)}, u32[]{:S(2)}) collective-permute-start(bf16[3120,128]{1,0:T(8,128)(2,1)S(1)} %pad_maximum_fusion.2.refs_0_), channel_id=1, source_target_pairs={{0,4},{1,5},{2,6},{3,7},{4,0},{5,1},{6,2},{7,3},{8,12},{9,13},{10,... | collective-permute-start | bytes 2396168 | tf_op jit(solution)/shard_map/ppermute | solution.py:333
  50.4 6.6 %collective-permute-start.14 = (bf16[3120,128]{1,0:T(8,128)(2,1)S(1)}, bf16[3120,128]{1,0:T(8,128)(2,1)S(1)}, u32[]{:S(2)}, u32[]{:S(2)}) collective-permute-start(bf16[3120,128]{1,0:T(8,128)(2,1)S(1)} %constant_dynamic-update-slice_fusion.refs_0_), channel_id=1, source_target_pairs={{0,4},{1,5},{2,6},{3,7},{4,0},{5,1},{6,2},{7,3},{8,12},{9,13},{10,... | collective-permute-start | bytes 2396168 | tf_op jit(solution)/shard_map/ppermute | solution.py:333
  50.5 8.5 %collective-permute-start.7 = (bf16[1040,128]{1,0:T(8,128)(2,1)S(1)}, bf16[1040,128]{1,0:T(8,128)(2,1)S(1)}, u32[]{:S(2)}, u32[]{:S(2)}) collective-permute-start(bf16[1040,128]{1,0:T(8,128)(2,1)S(1)} %collective-permute-done.5), channel_id=1, source_target_pairs={{0,8},{1,9},{2,10},{3,11},{4,12},{5,13},{6,14},{7,15},{8,24},{9,25... | collective-permute-start | bytes 798728 | tf_op jit(solution)/shard_map/ppermute | solution.py:333
  53.2 5.6 %collective-permute-start.18 = (bf16[1040,128]{1,0:T(8,128)(2,1)S(1)}, bf16[1040,128]{1,0:T(8,128)(2,1)S(1)}, u32[]{:S(2)}, u32[]{:S(2)}) collective-permute-start(bf16[1040,128]{1,0:T(8,128)(2,1)S(1)} %collective-permute-done.12), channel_id=1, source_target_pairs={{0,2},{1,3},{2,0},{3,1},{4,5},{5,4},{6,7},{7,6},{8,10},{9,11},{10,... | collective-permute-start | bytes 798728 | tf_op jit(solution)/shard_map/ppermute | solution.py:333
  59.0 5.6 %collective-permute-start.19 = (bf16[2080,128]{1,0:T(8,128)(2,1)S(1)}, bf16[2080,128]{1,0:T(8,128)(2,1)S(1)}, u32[]{:S(2)}, u32[]{:S(2)}) collective-permute-start(bf16[2080,128]{1,0:T(8,128)(2,1)S(1)} %constant_dynamic-update-slice_fusion.3.refs_0_), channel_id=1, source_target_pairs={{0,4},{1,5},{2,6},{3,7},{4,0},{5,1},{6,2},{7,3},{8,12},{9,13},{10,... | collective-permute-start | bytes 1597448 | tf_op jit(solution)/shard_map/ppermute | solution.py:333

commit v3 on v1

--- a/solution.py
+++ b/solution.py
@@ -281,8 +281,8 @@
             input_output_aliases=aliases,
             compiler_params=pltpu.CompilerParams(vmem_limit_bytes=28 * 1024 * 1024),
             cost_estimate=pl.CostEstimate(
-                flops=count * RUN * self.q.size * 4,
-                bytes_accessed=self.q.size * 8,
+                flops=1 * count * RUN * self.q.size * 4,
+                bytes_accessed=self.q.size * 8 * 1,
                 transcendentals=0,
             ),
             name=name,
@@ -373,44 +373,34 @@
     attention = Attention(q, group, half, 2 * inner)
     state = attention.start(own)
 
-    single = [1 << step for step in range(bits)]
-    several = [m for m in range(1, inner) if m not in single]
-
-    stages = [own]
-    for n in range(1, chips):
-        stages.append(along_z(stages[-1]))
-    planes, ready = [], []
-    for n in range(chips):
-        stage = stages[n]
-        before = planes[n - 1] if n else {}
-        if n:
-            earlier = [before[m] for m in single]
-            if n > 1:
-                earlier += [planes[n - 2][m] for m in several]
-            if n > 2:
-                state = attention.add(state, ready[n - 3])
-                earlier.append(state[0])
-            stage = tied(stage, *earlier)
-        found = {0: stage}
-        for step in range(bits):
-            found[1 << step] = over_place(stage, step)
-        if n + 1 < chips:
-            wait_for = [stages[n + 1]] + ([state[0]] if n == 0 else [])
+    stage, waiting = own, None
+    for n in range(chips - 1):
+        following = along_z(stage)
+        found = [stage]
+        if n == 0:
+            ones = [over_place(stage, step) for step in range(bits)]
+            for step in range(bits):
+                there = [ones[step]]
+                for x in found[1:]:
+                    there.append(over_place(x, step))
+                if step:
+                    there[1] = over_place(tied(found[1], following, state[0]), step)
+                found += there
+            held = jnp.concatenate(found)
         else:
-            state = attention.add(state, ready[n - 2])
-            wait_for = [state[0]]
-        for m in several:
-            if n + 2 == chips:
-                found[m] = along_z(tied(before[m], *wait_for))
-            else:
-                top = m.bit_length() - 1
-                found[m] = over_place(tied(found[m - (1 << top)], *wait_for), top)
-        planes.append(found)
-        if n + 1 < chips:
-            held = jnp.concatenate([found[m] for m in range(inner)])
-            ready.append([(held, int(n == 0)), other_core(held)])
-    waiting = ready[-1]
-    *most, final = (found[m] for m in range(inner))
+            held = tied(stage, *ones, state[0]) if n == 1 else stage
+            for step in range(bits):
+                held = jnp.concatenate([held, over_place(held, step)])
+        if waiting:
+            state = attention.add(state, waiting)
+            held = tied(held, state[0])
+        waiting = [(held, int(n == 0)), other_core(held)]
+        stage = following
+
+    found = [stage]
+    for step in range(bits):
+        found += [over_place(x, step) for x in found]
+    *most, final = found
     most = jnp.concatenate(most)
     theirs = other_core(most)
     state = attention.add(state, waiting)

time: 70.8 us -> 64.4 us (0.910)
  the two profiles are of different devices: /device:TPU:1 before, /device:TPU:10 now
where the time goes in v3:
time: 64.4 us; the launch traced here: 63.4 us
  waiting for transfers between devices  24.6 us (38%)
  Pallas kernels  21 us (33%)
  starting transfers between devices  15.6 us (24%)
  local copies, waits for them, and re-layouts  1.51 us (2%)
    ppermute x18, waiting for transfers between devices, permute(): return lax.ppermute(x, AXES, pairs)  24.6 us
    pallas_call x7, Pallas kernels, call(): pl.pallas_call(kernel, out_shape=shapes, in_specs=[vmem] * len(operands),...  19 us
    ppermute x18, starting transfers between devices, permute(): return lax.ppermute(x, AXES, pairs)  15.6 us
    pallas_call x1, Pallas kernels, per_device(): pl.pallas_call(pack_kernel, out_shape=jax.ShapeDtypeStruct((2 * tokens *...  2.07 us
    reshape x1, local copies, waits for them, and re-layouts, per_device(): queries.reshape(2, RUN, heads_kv, group, head_dim).transpose(0, 2, 1, 3, 4)  1.41 us
  transfers between devices with their start and end apart: 18, of which 6 were waited for; matrix products, arithmetic and copies ran while one was open for 3% of the time, Pallas kernels for 26%

profile of v3, /device:TPU:10, one launch (start us, length us, event | category | flops | bytes accessed | tf_op | source)
XLA Modules:
  0.0 63.4 jit_solution(14945687853248857623)
XLA Ops:
  0.0 2.1 %pack.1.own_ref = bf16[1040,128]{1,0:T(8,128)(2,1)} custom-call(bf16[512,128]{1,0:T(8,128)(2,1)} %bitcast.17, bf16[512,128]{1,0:T(8,128)(2,1)} %bitcast.18, s32[1,128]{1,0:T(1,128)} %bitcast.19), custom_call_target="tpu_custom_call" | custom-call | tf_op jit(solution)/shard_map/pack/pallas_call | solution.py:351
  2.1 0.0 copy-start
  2.1 2.6 %collective-permute-start = (bf16[1040,128]{1,0:T(8,128)(2,1)}, bf16[1040,128]{1,0:T(8,128)(2,1)S(1)}, u32[]{:S(2)}, u32[]{:S(2)}) collective-permute-start(bf16[1040,128]{1,0:T(8,128)(2,1)} %pack.1.own_ref), channel_id=1, source_target_pairs={{0,8},{1,9},{2,10},{3,11},{4,12},{5,13},{6,14},{7,15},{8,24},{9,25... | collective-permute-start | bytes 798728 | tf_op jit(solution)/shard_map/ppermute | solution.py:333
  4.7 0.5 collective-permute-start.9
  5.3 1.5 %collective-permute-start.10 = (bf16[1040,128]{1,0:T(8,128)(2,1)}, bf16[1040,128]{1,0:T(8,128)(2,1)S(1)}, u32[]{:S(2)}, u32[]{:S(2)}) collective-permute-start(bf16[1040,128]{1,0:T(8,128)(2,1)} %pack.1.own_ref), channel_id=1, source_target_pairs={{0,2},{1,3},{2,0},{3,1},{4,5},{5,4},{6,7},{7,6},{8,10},{9,11},{10,... | collective-permute-start | bytes 798728 | tf_op jit(solution)/shard_map/ppermute | solution.py:333
  6.8 1.4 %copy.37 = bf16[2,64,4,8,128]{4,3,1,2,0:T(8,128)(2,1)S(1)} copy(bf16[2,64,4,8,128]{4,3,2,1,0:T(8,128)(2,1)} %bitcast.16) | data formatting | bytes 2097152 | tf_op jit(solution)/shard_map/reshape | solution.py:368
  8.2 1.2 %attend_own.1 = (f32[8,128]{1,0:T(8,128)S(1)}, f32[2,4,512,128]{3,2,1,0:T(8,128)S(1)}, f32[2,4,512,128]{3,2,1,0:T(8,128)S(1)}, f32[2,4,512,128]{3,2,1,0:T(8,128)S(1)}, bf16[2,20,512,128]{3,2,1,0:T(8,128)(2,1)S(1)}) custom-call(bf16[2,4,512,128]{3,2,1,0:T(8,128)(2,1)S(1)} %bitcast.9, bf16[1040,128]{1,0:T(8,128)(2,1)S(1)} %copy-done), custom_call_target="tpu_custom_call" | custom-call | flops 268435456 | bytes 4194304 | tf_op jit(solution)/shard_map/attend_own/pallas_call | solution.py:275
  9.4 1.3 %collective-permute-done = bf16[1040,128]{1,0:T(8,128)(2,1)S(1)} collective-permute-done((bf16[1040,128]{1,0:T(8,128)(2,1)}, bf16[1040,128]{1,0:T(8,128)(2,1)S(1)}, u32[]{:S(2)}, u32[]{:S(2)}) %collective-permute-start) | collective-permute-done | bytes 266272 | tf_op jit(solution)/shard_map/ppermute | solution.py:333
  10.7 3.3 %collective-permute-done.9 = bf16[1040,128]{1,0:T(8,128)(2,1)S(1)} collective-permute-done((bf16[1040,128]{1,0:T(8,128)(2,1)}, bf16[1040,128]{1,0:T(8,128)(2,1)S(1)}, u32[]{:S(2)}, u32[]{:S(2)}) %collective-permute-start.9) | collective-permute-done | bytes 266272 | tf_op jit(solution)/shard_map/ppermute | solution.py:333
  14.0 0.0 collective-permute-done.10
  14.0 0.5 collective-permute-start.11
  14.6 0.5 collective-permute-start.13
  15.1 1.0 %collective-permute-start.1 = (bf16[1040,128]{1,0:T(8,128)(2,1)S(1)}, bf16[1040,128]{1,0:T(8,128)(2,1)S(1)}, u32[]{:S(2)}, u32[]{:S(2)}) collective-permute-start(bf16[1040,128]{1,0:T(8,128)(2,1)S(1)} %collective-permute-done), channel_id=1, source_target_pairs={{0,8},{1,9},{2,10},{3,11},{4,12},{5,13},{6,14},{7,15},{8,24},{9,25... | collective-permute-start | bytes 798728 | tf_op jit(solution)/shard_map/ppermute | solution.py:333
  16.0 6.2 %collective-permute-done.11 = bf16[1040,128]{1,0:T(8,128)(2,1)S(1)} collective-permute-done((bf16[1040,128]{1,0:T(8,128)(2,1)S(1)}, bf16[1040,128]{1,0:T(8,128)(2,1)S(1)}, u32[]{:S(2)}, u32[]{:S(2)}) %collective-permute-start.11) | collective-permute-done | bytes 266272 | tf_op jit(solution)/shard_map/ppermute | solution.py:333
  22.3 1.4 %collective-permute-start.12 = (bf16[2080,128]{1,0:T(8,128)(2,1)S(1)}, bf16[2080,128]{1,0:T(8,128)(2,1)S(1)}, u32[]{:S(2)}, u32[]{:S(2)}) collective-permute-start(bf16[2080,128]{1,0:T(8,128)(2,1)S(1)} %pad_maximum_fusion.4), channel_id=1, source_target_pairs={{0,2},{1,3},{2,0},{3,1},{4,5},{5,4},{6,7},{7,6},{8,10},{9,11},{10,... | collective-permute-start | bytes 1597448 | tf_op jit(solution)/shard_map/ppermute | solution.py:333
  23.7 0.0 collective-permute-done.1
  23.7 0.5 collective-permute-start.7
  24.3 0.0 collective-permute-done.13
  24.3 0.1 pad_maximum_fusion.2.refs_0_
  24.3 0.1 collective-permute-start.14
  24.4 1.2 %collective-permute-start.2 = (bf16[1040,128]{1,0:T(8,128)(2,1)S(1)}, bf16[1040,128]{1,0:T(8,128)(2,1)S(1)}, u32[]{:S(2)}, u32[]{:S(2)}) collective-permute-start(bf16[1040,128]{1,0:T(8,128)(2,1)S(1)} %collective-permute-done.1), channel_id=1, source_target_pairs={{0,8},{1,9},{2,10},{3,11},{4,12},{5,13},{6,14},{7,15},{8,24},{9,25... | collective-permute-start | bytes 798728 | tf_op jit(solution)/shard_map/ppermute | solution.py:333
  25.6 7.4 %collective-permute-done.7 = bf16[1040,128]{1,0:T(8,128)(2,1)S(1)} collective-permute-done((bf16[1040,128]{1,0:T(8,128)(2,1)S(1)}, bf16[1040,128]{1,0:T(8,128)(2,1)S(1)}, u32[]{:S(2)}, u32[]{:S(2)}) %collective-permute-start.7) | collective-permute-done | bytes 266272 | tf_op jit(solution)/shard_map/ppermute | solution.py:333
  33.1 0.1 collective-permute-start.8
  33.2 0.0 collective-permute-done.12
  33.2 0.1 pad_maximum_fusion.1.refs_0_
  33.3 0.0 collective-permute-done.14.refs_1_
  33.3 3.5 %attend.6 = (f32[8,128]{1,0:T(8,128)S(1)}, f32[2,4,512,128]{3,2,1,0:T(8,128)S(1)}, f32[2,4,512,128]{3,2,1,0:T(8,128)S(1)}, f32[2,4,512,128]{3,2,1,0:T(8,128)S(1)}, bf16[2,20,512,128]{3,2,1,0:T(8,128)(2,1)S(1)}) custom-call(bf16[2,4,512,128]{3,2,1,0:T(8,128)(2,1)S(1)} %bitcast.10, ...), custom_call_target="tpu_custom_call", output_to_operand_aliasing={{0}: (3, {}), {1}: (4, {}), {2}: (5, {}), {3}: (6, {}), {4}... | custom-call | flops 939524096 | bytes 4194304 | tf_op jit(solution)/shard_map/attend/pallas_call | solution.py:275
  36.8 0.1 collective-permute-start.15
  36.8 0.0 collective-permute-done.2
  36.9 0.1 collective-permute-start.3
  36.9 2.9 %collective-permute-start.5 = (bf16[1040,128]{1,0:T(8,128)(2,1)S(1)}, bf16[1040,128]{1,0:T(8,128)(2,1)S(1)}, u32[]{:S(2)}, u32[]{:S(2)}) collective-permute-start(bf16[1040,128]{1,0:T(8,128)(2,1)S(1)} %collective-permute-done.2), channel_id=1, source_target_pairs={{0,2},{1,3},{2,0},{3,1},{4,5},{5,4},{6,7},{7,6},{8,10},{9,11},{10,... | collective-permute-start | bytes 798728 | tf_op jit(solution)/shard_map/ppermute | solution.py:333
  39.9 5.0 %collective-permute-done.8 = bf16[2080,128]{1,0:T(8,128)(2,1)S(1)} collective-permute-done((bf16[2080,128]{1,0:T(8,128)(2,1)S(1)}, bf16[2080,128]{1,0:T(8,128)(2,1)S(1)}, u32[]{:S(2)}, u32[]{:S(2)}) %collective-permute-start.8) | collective-permute-done | bytes 532512 | tf_op jit(solution)/shard_map/ppermute | solution.py:333
  44.9 0.1 pad_maximum_fusion.refs_0_
  44.9 0.0 collective-permute-done.15.refs_1_
  44.9 1.8 %attend.7 = (f32[8,128]{1,0:T(8,128)S(1)}, f32[2,4,512,128]{3,2,1,0:T(8,128)S(1)}, f32[2,4,512,128]{3,2,1,0:T(8,128)S(1)}, f32[2,4,512,128]{3,2,1,0:T(8,128)S(1)}, bf16[2,20,512,128]{3,2,1,0:T(8,128)(2,1)S(1)}) custom-call(bf16[2,4,512,128]{3,2,1,0:T(8,128)(2,1)S(1)} %bitcast.11, ...), custom_call_target="tpu_custom_call", output_to_operand_aliasing={{0}: (3, {}), {1}: (4, {}), {2}: (5, {}), {3}: (6, {}), {4}... | custom-call | flops 1073741824 | bytes 4194304 | tf_op jit(solution)/shard_map/attend/pallas_call | solution.py:275
  46.7 0.1 collective-permute-start.16
  46.8 0.0 collective-permute-done.3
  46.9 1.3 %collective-permute-done.5 = bf16[1040,128]{1,0:T(8,128)(2,1)S(1)} collective-permute-done((bf16[1040,128]{1,0:T(8,128)(2,1)S(1)}, bf16[1040,128]{1,0:T(8,128)(2,1)S(1)}, u32[]{:S(2)}, u32[]{:S(2)}) %collective-permute-start.5) | collective-permute-done | bytes 266272 | tf_op jit(solution)/shard_map/ppermute | solution.py:333
  48.2 0.1 collective-permute-start.6
  48.3 2.3 %collective-permute-start.4 = (bf16[1040,128]{1,0:T(8,128)(2,1)S(1)}, bf16[1040,128]{1,0:T(8,128)(2,1)S(1)}, u32[]{:S(2)}, u32[]{:S(2)}) collective-permute-start(bf16[1040,128]{1,0:T(8,128)(2,1)S(1)} %collective-permute-done.3), channel_id=1, source_target_pairs={{0,2},{1,3},{2,0},{3,1},{4,5},{5,4},{6,7},{7,6},{8,10},{9,11},{10,... | collective-permute-start | bytes 798728 | tf_op jit(solution)/shard_map/ppermute | solution.py:333
  50.6 0.0 collective-permute-done.16.refs_1_
  50.6 3.8 %attend.8 = (f32[8,128]{1,0:T(8,128)S(1)}, f32[2,4,512,128]{3,2,1,0:T(8,128)S(1)}, f32[2,4,512,128]{3,2,1,0:T(8,128)S(1)}, f32[2,4,512,128]{3,2,1,0:T(8,128)S(1)}, bf16[2,20,512,128]{3,2,1,0:T(8,128)(2,1)S(1)}) custom-call(bf16[2,4,512,128]{3,2,1,0:T(8,128)(2,1)S(1)} %bitcast.12, ...), custom_call_target="tpu_custom_call", output_to_operand_aliasing={{0}: (3, {}), {1}: (4, {}), {2}: (5, {}), {3}: (6, {}), {4}... | custom-call | flops 1073741824 | bytes 4194304 | tf_op jit(solution)/shard_map/attend/pallas_call | solution.py:275
  54.4 0.0 collective-permute-done.6.refs_1_
  54.4 2.9 %attend.9 = (f32[8,128]{1,0:T(8,128)S(1)}, f32[2,4,512,128]{3,2,1,0:T(8,128)S(1)}, f32[2,4,512,128]{3,2,1,0:T(8,128)S(1)}, f32[2,4,512,128]{3,2,1,0:T(8,128)S(1)}, bf16[2,20,512,128]{3,2,1,0:T(8,128)(2,1)S(1)}) custom-call(bf16[2,4,512,128]{3,2,1,0:T(8,128)(2,1)S(1)} %bitcast.13, ...), custom_call_target="tpu_custom_call", output_to_operand_aliasing={{0}: (3, {}), {1}: (4, {}), {2}: (5, {}), {3}: (6, {}), {4}... | custom-call | flops 805306368 | bytes 4194304 | tf_op jit(solution)/shard_map/attend/pallas_call | solution.py:275
  57.3 0.1 collective-permute-start.17
  57.4 3.4 %attend.10 = (f32[8,128]{1,0:T(8,128)S(1)}, f32[2,4,512,128]{3,2,1,0:T(8,128)S(1)}, f32[2,4,512,128]{3,2,1,0:T(8,128)S(1)}, f32[2,4,512,128]{3,2,1,0:T(8,128)S(1)}, bf16[2,20,512,128]{3,2,1,0:T(8,128)(2,1)S(1)}) custom-call(bf16[2,4,512,128]{3,2,1,0:T(8,128)(2,1)S(1)} %bitcast.14, ...), custom_call_target="tpu_custom_call", output_to_operand_aliasing={{0}: (2, {}), {1}: (3, {}), {2}: (4, {}), {3}: (5, {}), {4}... | custom-call | flops 134217728 | bytes 4194304 | tf_op jit(solution)/shard_map/attend/pallas_call | solution.py:275
  60.8 0.0 collective-permute-done.17.refs_0_
  60.8 2.4 %attend.11 = (bf16[128,32,128]{2,1,0:T(8,128)(2,1)}, f32[8,128]{1,0:T(8,128)S(1)}, f32[2,4,512,128]{3,2,1,0:T(8,128)S(1)}, f32[2,4,512,128]{3,2,1,0:T(8,128)S(1)...) custom-call(bf16[2,4,512,128]{3,2,1,0:T(8,128)(2,1)S(1)} %bitcast.15, ...), custom_call_target="tpu_custom_call", output_to_operand_aliasing={{1}: (2, {}), {2}: (3, {}), {3}: (4, {}), {4}: (5, {}), {5}... | custom-call | flops 134217728 | bytes 4194304 | tf_op jit(solution)/shard_map/attend/pallas_call | solution.py:275
  (7 shorter events, 0.2 us)
Async XLA Ops:
  2.1 6.1 %copy-start = (bf16[1040,128]{1,0:T(8,128)(2,1)S(1)}, bf16[1040,128]{1,0:T(8,128)(2,1)}, u32[]{:S(2)}) copy-start(bf16[1040,128]{1,0:T(8,128)(2,1)} %pack.1.own_ref) | copy-start | bytes 798724
  2.1 8.6 %collective-permute-start = (bf16[1040,128]{1,0:T(8,128)(2,1)}, bf16[1040,128]{1,0:T(8,128)(2,1)S(1)}, u32[]{:S(2)}, u32[]{:S(2)}) collective-permute-start(bf16[1040,128]{1,0:T(8,128)(2,1)} %pack.1.own_ref), channel_id=1, source_target_pairs={{0,8},{1,9},{2,10},{3,11},{4,12},{5,13},{6,14},{7,15},{8,24},{9,25... | collective-permute-start | bytes 798728 | tf_op jit(solution)/shard_map/ppermute | solution.py:333
  4.7 9.3 %collective-permute-start.9 = (bf16[1040,128]{1,0:T(8,128)(2,1)}, bf16[1040,128]{1,0:T(8,128)(2,1)S(1)}, u32[]{:S(2)}, u32[]{:S(2)}) collective-permute-start(bf16[1040,128]{1,0:T(8,128)(2,1)} %pack.1.own_ref), channel_id=1, source_target_pairs={{0,1},{1,0},{2,3},{3,2},{4,6},{5,7},{6,4},{7,5},{8,9},{9,8},{10,11... | collective-permute-start | bytes 798728 | tf_op jit(solution)/shard_map/ppermute | solution.py:333
  5.3 8.8 %collective-permute-start.10 = (bf16[1040,128]{1,0:T(8,128)(2,1)}, bf16[1040,128]{1,0:T(8,128)(2,1)S(1)}, u32[]{:S(2)}, u32[]{:S(2)}) collective-permute-start(bf16[1040,128]{1,0:T(8,128)(2,1)} %pack.1.own_ref), channel_id=1, source_target_pairs={{0,2},{1,3},{2,0},{3,1},{4,5},{5,4},{6,7},{7,6},{8,10},{9,11},{10,... | collective-permute-start | bytes 798728 | tf_op jit(solution)/shard_map/ppermute | solution.py:333
  14.0 8.2 %collective-permute-start.11 = (bf16[1040,128]{1,0:T(8,128)(2,1)S(1)}, bf16[1040,128]{1,0:T(8,128)(2,1)S(1)}, u32[]{:S(2)}, u32[]{:S(2)}) collective-permute-start(bf16[1040,128]{1,0:T(8,128)(2,1)S(1)} %collective-permute-done), channel_id=1, source_target_pairs={{0,1},{1,0},{2,3},{3,2},{4,6},{5,7},{6,4},{7,5},{8,9},{9,8},{10,11... | collective-permute-start | bytes 798728 | tf_op jit(solution)/shard_map/ppermute | solution.py:333
  14.6 9.7 %collective-permute-start.13 = (bf16[1040,128]{1,0:T(8,128)(2,1)S(1)}, bf16[1040,128]{1,0:T(8,128)(2,1)S(1)}, u32[]{:S(2)}, u32[]{:S(2)}) collective-permute-start(bf16[1040,128]{1,0:T(8,128)(2,1)S(1)} %collective-permute-done.9), channel_id=1, source_target_pairs={{0,2},{1,3},{2,0},{3,1},{4,5},{5,4},{6,7},{7,6},{8,10},{9,11},{10,... | collective-permute-start | bytes 798728 | tf_op jit(solution)/shard_map/ppermute | solution.py:333
  15.1 8.6 %collective-permute-start.1 = (bf16[1040,128]{1,0:T(8,128)(2,1)S(1)}, bf16[1040,128]{1,0:T(8,128)(2,1)S(1)}, u32[]{:S(2)}, u32[]{:S(2)}) collective-permute-start(bf16[1040,128]{1,0:T(8,128)(2,1)S(1)} %collective-permute-done), channel_id=1, source_target_pairs={{0,8},{1,9},{2,10},{3,11},{4,12},{5,13},{6,14},{7,15},{8,24},{9,25... | collective-permute-start | bytes 798728 | tf_op jit(solution)/shard_map/ppermute | solution.py:333
  22.3 10.9 %collective-permute-start.12 = (bf16[2080,128]{1,0:T(8,128)(2,1)S(1)}, bf16[2080,128]{1,0:T(8,128)(2,1)S(1)}, u32[]{:S(2)}, u32[]{:S(2)}) collective-permute-start(bf16[2080,128]{1,0:T(8,128)(2,1)S(1)} %pad_maximum_fusion.4), channel_id=1, source_target_pairs={{0,2},{1,3},{2,0},{3,1},{4,5},{5,4},{6,7},{7,6},{8,10},{9,11},{10,... | collective-permute-start | bytes 1597448 | tf_op jit(solution)/shard_map/ppermute | solution.py:333
  23.7 9.3 %collective-permute-start.7 = (bf16[1040,128]{1,0:T(8,128)(2,1)S(1)}, bf16[1040,128]{1,0:T(8,128)(2,1)S(1)}, u32[]{:S(2)}, u32[]{:S(2)}) collective-permute-start(bf16[1040,128]{1,0:T(8,128)(2,1)S(1)} %collective-permute-done.1), channel_id=1, source_target_pairs={{0,1},{1,0},{2,3},{3,2},{4,6},{5,7},{6,4},{7,5},{8,9},{9,8},{10,11... | collective-permute-start | bytes 798728 | tf_op jit(solution)/shard_map/ppermute | solution.py:333
  24.3 8.9 %collective-permute-start.14 = (bf16[4160,128]{1,0:T(8,128)(2,1)S(1)}, bf16[4160,128]{1,0:T(8,128)(2,1)S(1)}, u32[]{:S(2)}, u32[]{:S(2)}) collective-permute-start(bf16[4160,128]{1,0:T(8,128)(2,1)S(1)} %pad_maximum_fusion.2.refs_0_), channel_id=1, source_target_pairs={{0,4},{1,5},{2,6},{3,7},{4,0},{5,1},{6,2},{7,3},{8,12},{9,13},{10,... | collective-permute-start | bytes 3194888 | tf_op jit(solution)/shard_map/ppermute | solution.py:333
  24.4 12.4 %collective-permute-start.2 = (bf16[1040,128]{1,0:T(8,128)(2,1)S(1)}, bf16[1040,128]{1,0:T(8,128)(2,1)S(1)}, u32[]{:S(2)}, u32[]{:S(2)}) collective-permute-start(bf16[1040,128]{1,0:T(8,128)(2,1)S(1)} %collective-permute-done.1), channel_id=1, source_target_pairs={{0,8},{1,9},{2,10},{3,11},{4,12},{5,13},{6,14},{7,15},{8,24},{9,25... | collective-permute-start | bytes 798728 | tf_op jit(solution)/shard_map/ppermute | solution.py:333
  33.1 11.8 %collective-permute-start.8 = (bf16[2080,128]{1,0:T(8,128)(2,1)S(1)}, bf16[2080,128]{1,0:T(8,128)(2,1)S(1)}, u32[]{:S(2)}, u32[]{:S(2)}) collective-permute-start(bf16[2080,128]{1,0:T(8,128)(2,1)S(1)} %pad_maximum_fusion.3), channel_id=1, source_target_pairs={{0,2},{1,3},{2,0},{3,1},{4,5},{5,4},{6,7},{7,6},{8,10},{9,11},{10,... | collective-permute-start | bytes 1597448 | tf_op jit(solution)/shard_map/ppermute | solution.py:333
  36.8 8.2 %collective-permute-start.15 = (bf16[4160,128]{1,0:T(8,128)(2,1)S(1)}, bf16[4160,128]{1,0:T(8,128)(2,1)S(1)}, u32[]{:S(2)}, u32[]{:S(2)}) collective-permute-start(bf16[4160,128]{1,0:T(8,128)(2,1)S(1)} %pad_maximum_fusion.1.refs_0_), channel_id=1, source_target_pairs={{0,4},{1,5},{2,6},{3,7},{4,0},{5,1},{6,2},{7,3},{8,12},{9,13},{10,... | collective-permute-start | bytes 3194888 | tf_op jit(solution)/shard_map/ppermute | solution.py:333
  36.9 9.9 %collective-permute-start.3 = (bf16[1040,128]{1,0:T(8,128)(2,1)S(1)}, bf16[1040,128]{1,0:T(8,128)(2,1)S(1)}, u32[]{:S(2)}, u32[]{:S(2)}) collective-permute-start(bf16[1040,128]{1,0:T(8,128)(2,1)S(1)} %collective-permute-done.2), channel_id=1, source_target_pairs={{0,1},{1,0},{2,3},{3,2},{4,6},{5,7},{6,4},{7,5},{8,9},{9,8},{10,11... | collective-permute-start | bytes 798728 | tf_op jit(solution)/shard_map/ppermute | solution.py:333
  36.9 11.2 %collective-permute-start.5 = (bf16[1040,128]{1,0:T(8,128)(2,1)S(1)}, bf16[1040,128]{1,0:T(8,128)(2,1)S(1)}, u32[]{:S(2)}, u32[]{:S(2)}) collective-permute-start(bf16[1040,128]{1,0:T(8,128)(2,1)S(1)} %collective-permute-done.2), channel_id=1, source_target_pairs={{0,2},{1,3},{2,0},{3,1},{4,5},{5,4},{6,7},{7,6},{8,10},{9,11},{10,... | collective-permute-start | bytes 798728 | tf_op jit(solution)/shard_map/ppermute | solution.py:333
  46.7 3.9 %collective-permute-start.16 = (bf16[4160,128]{1,0:T(8,128)(2,1)S(1)}, bf16[4160,128]{1,0:T(8,128)(2,1)S(1)}, u32[]{:S(2)}, u32[]{:S(2)}) collective-permute-start(bf16[4160,128]{1,0:T(8,128)(2,1)S(1)} %pad_maximum_fusion.refs_0_), channel_id=1, source_target_pairs={{0,4},{1,5},{2,6},{3,7},{4,0},{5,1},{6,2},{7,3},{8,12},{9,13},{10,... | collective-permute-start | bytes 3194888 | tf_op jit(solution)/shard_map/ppermute | solution.py:333
  48.2 6.2 %collective-permute-start.6 = (bf16[3120,128]{1,0:T(8,128)(2,1)S(1)}, bf16[3120,128]{1,0:T(8,128)(2,1)S(1)}, u32[]{:S(2)}, u32[]{:S(2)}) collective-permute-start(bf16[3120,128]{1,0:T(8,128)(2,1)S(1)} %constant_dynamic-update-slice_fusion.refs_0_), channel_id=1, source_target_pairs={{0,4},{1,5},{2,6},{3,7},{4,0},{5,1},{6,2},{7,3},{8,12},{9,13},{10,... | collective-permute-start | bytes 2396168 | tf_op jit(solution)/shard_map/ppermute | solution.py:333
  48.3 9.0 %collective-permute-start.4 = (bf16[1040,128]{1,0:T(8,128)(2,1)S(1)}, bf16[1040,128]{1,0:T(8,128)(2,1)S(1)}, u32[]{:S(2)}, u32[]{:S(2)}) collective-permute-start(bf16[1040,128]{1,0:T(8,128)(2,1)S(1)} %collective-permute-done.3), channel_id=1, source_target_pairs={{0,2},{1,3},{2,0},{3,1},{4,5},{5,4},{6,7},{7,6},{8,10},{9,11},{10,... | collective-permute-start | bytes 798728 | tf_op jit(solution)/shard_map/ppermute | solution.py:333
  57.3 3.5 %collective-permute-start.17 = (bf16[1040,128]{1,0:T(8,128)(2,1)S(1)}, bf16[1040,128]{1,0:T(8,128)(2,1)S(1)}, u32[]{:S(2)}, u32[]{:S(2)}) collective-permute-start(bf16[1040,128]{1,0:T(8,128)(2,1)S(1)} %collective-permute-done.4.refs_0_), channel_id=1, source_target_pairs={{0,4},{1,5},{2,6},{3,7},{4,0},{5,1},{6,2},{7,3},{8,12},{9,13},{10,... | collective-permute-start | bytes 798728 | tf_op jit(solution)/shard_map/ppermute | solution.py:333

commit v4 on v3

--- a/solution.py
+++ b/solution.py
@@ -373,9 +373,11 @@
     attention = Attention(q, group, half, 2 * inner)
     state = attention.start(own)
 
-    stage, waiting = own, None
-    for n in range(chips - 1):
-        following = along_z(stage)
+    stages = [own]
+    for n in range(1, chips):
+        stages.append(along_z(stages[-1]))
+    todo = []
+    for n, stage in enumerate(stages[:-1]):
         found = [stage]
         if n == 0:
             ones = [over_place(stage, step) for step in range(bits)]
@@ -384,27 +386,28 @@
                 for x in found[1:]:
                     there.append(over_place(x, step))
                 if step:
-                    there[1] = over_place(tied(found[1], following, state[0]), step)
+                    there[1] = over_place(tied(found[1], stages[1], state[0]), step)
                 found += there
             held = jnp.concatenate(found)
         else:
             held = tied(stage, *ones, state[0]) if n == 1 else stage
             for step in range(bits):
-                held = jnp.concatenate([held, over_place(held, step)])
-        if waiting:
-            state = attention.add(state, waiting)
-            held = tied(held, state[0])
-        waiting = [(held, int(n == 0)), other_core(held)]
-        stage = following
-
-    found = [stage]
+                there = over_place(held, step)
+                if todo and (step == 0 and n > 1 or step + 1 == bits and n + 2 == chips):
+                    state = attention.add(state, todo.pop(0))
+                    there = tied(there, state[0])
+                held = jnp.concatenate([held, there])
+        theirs = other_core(held)
+        todo.append([(held, int(n == 0)), theirs])
+
+    found = [stages[-1]]
     for step in range(bits):
         found += [over_place(x, step) for x in found]
     *most, final = found
+    mine, theirs = todo.pop()
     most = jnp.concatenate(most)
-    theirs = other_core(most)
-    state = attention.add(state, waiting)
-    state = attention.add(state, [most, theirs])
+    state = attention.add(state, [mine, most])
+    state = attention.add(state, [theirs, other_core(most)])
     final = tied(final, state[0])
     theirs = other_core(final)
     state = attention.add(state, [final], keep=1)

time: 64.4 us -> 64.9 us (level)
  the two profiles are of different devices: /device:TPU:10 before, /device:TPU:1 now
where the time goes in v4:
time: 64.9 us; the launch traced here: 63.7 us
  starting transfers between devices  30.3 us (47%)
  waiting for transfers between devices  22.8 us (35%)
  Pallas kernels  8.26 us (13%)
  local copies, waits for them, and re-layouts  1.76 us (3%)
    ppermute x18, starting transfers between devices, permute(): return lax.ppermute(x, AXES, pairs)  30.3 us
    ppermute x18, waiting for transfers between devices, permute(): return lax.ppermute(x, AXES, pairs)  22.8 us
    pallas_call x7, Pallas kernels, call(): pl.pallas_call(kernel, out_shape=shapes, in_specs=[vmem] * len(operands),...  6.19 us
    pallas_call x1, Pallas kernels, per_device(): pl.pallas_call(pack_kernel, out_shape=jax.ShapeDtypeStruct((2 * tokens *...  2.08 us
    reshape x1, local copies, waits for them, and re-layouts, per_device(): queries.reshape(2, RUN, heads_kv, group, head_dim).transpose(0, 2, 1, 3, 4)  1.41 us
  transfers between devices with their start and end apart: 18, of which 8 were waited for; matrix products, arithmetic and copies ran while one was open for 3% of the time, Pallas kernels for 7%

profile of v4, /device:TPU:1, one launch (start us, length us, event | category | flops | bytes accessed | tf_op | source)
XLA Modules:
  0.0 63.7 jit_solution(448622849431813919)
XLA Ops:
  0.0 2.1 %pack.1.own_ref = bf16[1040,128]{1,0:T(8,128)(2,1)} custom-call(bf16[512,128]{1,0:T(8,128)(2,1)} %bitcast.17, bf16[512,128]{1,0:T(8,128)(2,1)} %bitcast.18, s32[1,128]{1,0:T(1,128)} %bitcast.19), custom_call_target="tpu_custom_call" | custom-call | tf_op jit(solution)/shard_map/pack/pallas_call | solution.py:351
  2.1 0.0 copy-start
  2.1 2.2 %collective-permute-start = (bf16[1040,128]{1,0:T(8,128)(2,1)}, bf16[1040,128]{1,0:T(8,128)(2,1)S(1)}, u32[]{:S(2)}, u32[]{:S(2)}) collective-permute-start(bf16[1040,128]{1,0:T(8,128)(2,1)} %pack.1.own_ref), channel_id=1, source_target_pairs={{0,8},{1,9},{2,10},{3,11},{4,12},{5,13},{6,14},{7,15},{8,24},{9,25... | collective-permute-start | bytes 798728 | tf_op jit(solution)/shard_map/ppermute | solution.py:333
  4.3 1.2 %collective-permute-start.6 = (bf16[1040,128]{1,0:T(8,128)(2,1)}, bf16[1040,128]{1,0:T(8,128)(2,1)S(1)}, u32[]{:S(2)}, u32[]{:S(2)}) collective-permute-start(bf16[1040,128]{1,0:T(8,128)(2,1)} %pack.1.own_ref), channel_id=1, source_target_pairs={{0,1},{1,0},{2,3},{3,2},{4,6},{5,7},{6,4},{7,5},{8,9},{9,8},{10,11... | collective-permute-start | bytes 798728 | tf_op jit(solution)/shard_map/ppermute | solution.py:333
  5.5 1.2 %collective-permute-start.7 = (bf16[1040,128]{1,0:T(8,128)(2,1)}, bf16[1040,128]{1,0:T(8,128)(2,1)S(1)}, u32[]{:S(2)}, u32[]{:S(2)}) collective-permute-start(bf16[1040,128]{1,0:T(8,128)(2,1)} %pack.1.own_ref), channel_id=1, source_target_pairs={{0,2},{1,3},{2,0},{3,1},{4,5},{5,4},{6,7},{7,6},{8,10},{9,11},{10,... | collective-permute-start | bytes 798728 | tf_op jit(solution)/shard_map/ppermute | solution.py:333
  6.7 1.4 %copy.37 = bf16[2,64,4,8,128]{4,3,1,2,0:T(8,128)(2,1)S(1)} copy(bf16[2,64,4,8,128]{4,3,2,1,0:T(8,128)(2,1)} %bitcast.16) | data formatting | bytes 2097152 | tf_op jit(solution)/shard_map/reshape | solution.py:368
  8.2 1.2 %attend_own.1 = (f32[8,128]{1,0:T(8,128)S(1)}, f32[2,4,512,128]{3,2,1,0:T(8,128)S(1)}, f32[2,4,512,128]{3,2,1,0:T(8,128)S(1)}, f32[2,4,512,128]{3,2,1,0:T(8,128)S(1)}, bf16[2,20,512,128]{3,2,1,0:T(8,128)(2,1)S(1)}) custom-call(bf16[2,4,512,128]{3,2,1,0:T(8,128)(2,1)S(1)} %bitcast.9, bf16[1040,128]{1,0:T(8,128)(2,1)S(1)} %copy-done), custom_call_target="tpu_custom_call" | custom-call | flops 268435456 | bytes 4194304 | tf_op jit(solution)/shard_map/attend_own/pallas_call | solution.py:275
  9.3 2.3 %collective-permute-done = bf16[1040,128]{1,0:T(8,128)(2,1)S(1)} collective-permute-done((bf16[1040,128]{1,0:T(8,128)(2,1)}, bf16[1040,128]{1,0:T(8,128)(2,1)S(1)}, u32[]{:S(2)}, u32[]{:S(2)}) %collective-permute-start) | collective-permute-done | bytes 266272 | tf_op jit(solution)/shard_map/ppermute | solution.py:333
  11.6 0.0 collective-permute-done.6
  11.6 2.3 %collective-permute-done.7 = bf16[1040,128]{1,0:T(8,128)(2,1)S(1)} collective-permute-done((bf16[1040,128]{1,0:T(8,128)(2,1)}, bf16[1040,128]{1,0:T(8,128)(2,1)S(1)}, u32[]{:S(2)}, u32[]{:S(2)}) %collective-permute-start.7) | collective-permute-done | bytes 266272 | tf_op jit(solution)/shard_map/ppermute | solution.py:333
  14.0 0.0 collective-permute-start.11
  14.0 1.2 %collective-permute-start.8 = (bf16[1040,128]{1,0:T(8,128)(2,1)S(1)}, bf16[1040,128]{1,0:T(8,128)(2,1)S(1)}, u32[]{:S(2)}, u32[]{:S(2)}) collective-permute-start(bf16[1040,128]{1,0:T(8,128)(2,1)S(1)} %collective-permute-done.6), channel_id=1, source_target_pairs={{0,2},{1,3},{2,0},{3,1},{4,5},{5,4},{6,7},{7,6},{8,10},{9,11},{10,... | collective-permute-start | bytes 798728 | tf_op jit(solution)/shard_map/ppermute | solution.py:333
  15.2 2.3 %collective-permute-start.1 = (bf16[1040,128]{1,0:T(8,128)(2,1)S(1)}, bf16[1040,128]{1,0:T(8,128)(2,1)S(1)}, u32[]{:S(2)}, u32[]{:S(2)}) collective-permute-start(bf16[1040,128]{1,0:T(8,128)(2,1)S(1)} %collective-permute-done), channel_id=1, source_target_pairs={{0,8},{1,9},{2,10},{3,11},{4,12},{5,13},{6,14},{7,15},{8,24},{9,25... | collective-permute-start | bytes 798728 | tf_op jit(solution)/shard_map/ppermute | solution.py:333
  17.5 2.3 %collective-permute-done.11 = bf16[1040,128]{1,0:T(8,128)(2,1)S(1)} collective-permute-done((bf16[1040,128]{1,0:T(8,128)(2,1)S(1)}, bf16[1040,128]{1,0:T(8,128)(2,1)S(1)}, u32[]{:S(2)}, u32[]{:S(2)}) %collective-permute-start.11) | collective-permute-done | bytes 266272 | tf_op jit(solution)/shard_map/ppermute | solution.py:333
  19.8 2.2 %collective-permute-start.12 = (bf16[2080,128]{1,0:T(8,128)(2,1)S(1)}, bf16[2080,128]{1,0:T(8,128)(2,1)S(1)}, u32[]{:S(2)}, u32[]{:S(2)}) collective-permute-start(bf16[2080,128]{1,0:T(8,128)(2,1)S(1)} %pad_maximum_fusion.2), channel_id=1, source_target_pairs={{0,2},{1,3},{2,0},{3,1},{4,5},{5,4},{6,7},{7,6},{8,10},{9,11},{10,... | collective-permute-start | bytes 1597448 | tf_op jit(solution)/shard_map/ppermute | solution.py:333
  22.1 0.0 collective-permute-done.8
  22.1 0.1 pad_maximum_fusion.refs_0_
  22.1 2.2 %collective-permute-start.9 = (bf16[4160,128]{1,0:T(8,128)(2,1)S(1)}, bf16[4160,128]{1,0:T(8,128)(2,1)S(1)}, u32[]{:S(2)}, u32[]{:S(2)}) collective-permute-start(bf16[4160,128]{1,0:T(8,128)(2,1)S(1)} %pad_maximum_fusion.refs_0_), channel_id=1, source_target_pairs={{0,4},{1,5},{2,6},{3,7},{4,0},{5,1},{6,2},{7,3},{8,12},{9,13},{10,... | collective-permute-start | bytes 3194888 | tf_op jit(solution)/shard_map/ppermute | solution.py:333
  24.4 0.0 collective-permute-done.1
  24.4 0.5 collective-permute-start.5
  24.9 2.3 %collective-permute-start.2 = (bf16[1040,128]{1,0:T(8,128)(2,1)S(1)}, bf16[1040,128]{1,0:T(8,128)(2,1)S(1)}, u32[]{:S(2)}, u32[]{:S(2)}) collective-permute-start(bf16[1040,128]{1,0:T(8,128)(2,1)S(1)} %collective-permute-done.1), channel_id=1, source_target_pairs={{0,8},{1,9},{2,10},{3,11},{4,12},{5,13},{6,14},{7,15},{8,24},{9,25... | collective-permute-start | bytes 798728 | tf_op jit(solution)/shard_map/ppermute | solution.py:333
  27.2 2.7 %collective-permute-done.12 = bf16[2080,128]{1,0:T(8,128)(2,1)S(1)} collective-permute-done((bf16[2080,128]{1,0:T(8,128)(2,1)S(1)}, bf16[2080,128]{1,0:T(8,128)(2,1)S(1)}, u32[]{:S(2)}, u32[]{:S(2)}) %collective-permute-start.12) | collective-permute-done | bytes 532512 | tf_op jit(solution)/shard_map/ppermute | solution.py:333
  29.9 0.1 constant_dynamic-update-slice_fusion.refs_0_
  30.0 5.2 %collective-permute-start.13 = (bf16[4160,128]{1,0:T(8,128)(2,1)S(1)}, bf16[4160,128]{1,0:T(8,128)(2,1)S(1)}, u32[]{:S(2)}, u32[]{:S(2)}) collective-permute-start(bf16[4160,128]{1,0:T(8,128)(2,1)S(1)} %constant_dynamic-update-slice_fusion.refs_0_), channel_id=1, source_target_pairs={{0,4},{1,5},{2,6},{3,7},{4,0},{5,1},{6,2},{7,3},{8,12},{9,13},{10,... | collective-permute-start | bytes 3194888 | tf_op jit(solution)/shard_map/ppermute | solution.py:333
  35.2 0.0 collective-permute-done.2
  35.2 1.1 %collective-permute-start.3 = (bf16[1040,128]{1,0:T(8,128)(2,1)S(1)}, bf16[1040,128]{1,0:T(8,128)(2,1)S(1)}, u32[]{:S(2)}, u32[]{:S(2)}) collective-permute-start(bf16[1040,128]{1,0:T(8,128)(2,1)S(1)} %collective-permute-done.2), channel_id=1, source_target_pairs={{0,1},{1,0},{2,3},{3,2},{4,6},{5,7},{6,4},{7,5},{8,9},{9,8},{10,11... | collective-permute-start | bytes 798728 | tf_op jit(solution)/shard_map/ppermute | solution.py:333
  36.3 1.2 %collective-permute-start.15 = (bf16[1040,128]{1,0:T(8,128)(2,1)S(1)}, bf16[1040,128]{1,0:T(8,128)(2,1)S(1)}, u32[]{:S(2)}, u32[]{:S(2)}) collective-permute-start(bf16[1040,128]{1,0:T(8,128)(2,1)S(1)} %collective-permute-done.2), channel_id=1, source_target_pairs={{0,2},{1,3},{2,0},{3,1},{4,5},{5,4},{6,7},{7,6},{8,10},{9,11},{10,... | collective-permute-start | bytes 798728 | tf_op jit(solution)/shard_map/ppermute | solution.py:333
  37.5 0.0 collective-permute-done.9.refs_1_
  37.5 0.5 attend.6
  38.0 0.0 collective-permute-done.5
  38.1 1.5 %collective-permute-start.10 = (bf16[2080,128]{1,0:T(8,128)(2,1)S(1)}, bf16[2080,128]{1,0:T(8,128)(2,1)S(1)}, u32[]{:S(2)}, u32[]{:S(2)}) collective-permute-start(bf16[2080,128]{1,0:T(8,128)(2,1)S(1)} %pad_maximum_fusion.1), channel_id=1, source_target_pairs={{0,2},{1,3},{2,0},{3,1},{4,5},{5,4},{6,7},{7,6},{8,10},{9,11},{10,... | collective-permute-start | bytes 1597448 | tf_op jit(solution)/shard_map/ppermute | solution.py:333
  39.7 0.0 collective-permute-done.13.refs_1_
  39.7 0.6 attend.7
  40.3 9.6 %collective-permute-done.10 = bf16[2080,128]{1,0:T(8,128)(2,1)S(1)} collective-permute-done((bf16[2080,128]{1,0:T(8,128)(2,1)S(1)}, bf16[2080,128]{1,0:T(8,128)(2,1)S(1)}, u32[]{:S(2)}, u32[]{:S(2)}) %collective-permute-start.10) | collective-permute-done | bytes 532512 | tf_op jit(solution)/shard_map/ppermute | solution.py:333
  49.8 0.1 constant_dynamic-update-slice_fusion.3.refs_0_
  49.9 0.6 %collective-permute-start.14 = (bf16[4160,128]{1,0:T(8,128)(2,1)S(1)}, bf16[4160,128]{1,0:T(8,128)(2,1)S(1)}, u32[]{:S(2)}, u32[]{:S(2)}) collective-permute-start(bf16[4160,128]{1,0:T(8,128)(2,1)S(1)} %constant_dynamic-update-slice_fusion.3.refs_0_), channel_id=1, source_target_pairs={{0,4},{1,5},{2,6},{3,7},{4,0},{5,1},{6,2},{7,3},{8,12},{9,13},{10,... | collective-permute-start | bytes 3194888 | tf_op jit(solution)/shard_map/ppermute | solution.py:333
  50.6 0.0 collective-permute-done.3
  50.6 0.0 collective-permute-done.15
  50.7 0.1 collective-permute-start.16
  50.7 0.8 %collective-permute-start.4 = (bf16[1040,128]{1,0:T(8,128)(2,1)S(1)}, bf16[1040,128]{1,0:T(8,128)(2,1)S(1)}, u32[]{:S(2)}, u32[]{:S(2)}) collective-permute-start(bf16[1040,128]{1,0:T(8,128)(2,1)S(1)} %collective-permute-done.3), channel_id=1, source_target_pairs={{0,2},{1,3},{2,0},{3,1},{4,5},{5,4},{6,7},{7,6},{8,10},{9,11},{10,... | collective-permute-start | bytes 798728 | tf_op jit(solution)/shard_map/ppermute | solution.py:333
  51.6 0.7 %attend.8 = (f32[8,128]{1,0:T(8,128)S(1)}, f32[2,4,512,128]{3,2,1,0:T(8,128)S(1)}, f32[2,4,512,128]{3,2,1,0:T(8,128)S(1)}, f32[2,4,512,128]{3,2,1,0:T(8,128)S(1)}, bf16[2,20,512,128]{3,2,1,0:T(8,128)(2,1)S(1)}) custom-call(bf16[2,4,512,128]{3,2,1,0:T(8,128)(2,1)S(1)} %bitcast.12, ...), custom_call_target="tpu_custom_call", output_to_operand_aliasing={{0}: (3, {}), {1}: (4, {}), {2}: (5, {}), {3}: (6, {}), {4}... | custom-call | flops 939524096 | bytes 4194304 | tf_op jit(solution)/shard_map/attend/pallas_call | solution.py:275
  52.3 1.7 %collective-permute-done.16.refs_1_ = bf16[3120,128]{1,0:T(8,128)(2,1)S(1)} collective-permute-done((bf16[3120,128]{1,0:T(8,128)(2,1)S(1)}, bf16[3120,128]{1,0:T(8,128)(2,1)S(1)}, u32[]{:S(2)}, u32[]{:S(2)}) %collective-permute-start.16) | collective-permute-done | bytes 798752 | tf_op jit(solution)/shard_map/ppermute | solution.py:333
  54.0 0.5 attend.9
  54.5 1.8 %collective-permute-done.4.refs_0_ = bf16[1040,128]{1,0:T(8,128)(2,1)S(1)} collective-permute-done((bf16[1040,128]{1,0:T(8,128)(2,1)S(1)}, bf16[1040,128]{1,0:T(8,128)(2,1)S(1)}, u32[]{:S(2)}, u32[]{:S(2)}) %collective-permute-start.4) | collective-permute-done | bytes 266272 | tf_op jit(solution)/shard_map/ppermute | solution.py:333
  56.4 4.3 %collective-permute-start.17 = (bf16[1040,128]{1,0:T(8,128)(2,1)S(1)}, bf16[1040,128]{1,0:T(8,128)(2,1)S(1)}, u32[]{:S(2)}, u32[]{:S(2)}) collective-permute-start(bf16[1040,128]{1,0:T(8,128)(2,1)S(1)} %collective-permute-done.4.refs_0_), channel_id=1, source_target_pairs={{0,4},{1,5},{2,6},{3,7},{4,0},{5,1},{6,2},{7,3},{8,12},{9,13},{10,... | collective-permute-start | bytes 798728 | tf_op jit(solution)/shard_map/ppermute | solution.py:333
  60.7 1.0 %attend.10 = (f32[8,128]{1,0:T(8,128)S(1)}, f32[2,4,512,128]{3,2,1,0:T(8,128)S(1)}, f32[2,4,512,128]{3,2,1,0:T(8,128)S(1)}, f32[2,4,512,128]{3,2,1,0:T(8,128)S(1)}, bf16[2,20,512,128]{3,2,1,0:T(8,128)(2,1)S(1)}) custom-call(bf16[2,4,512,128]{3,2,1,0:T(8,128)(2,1)S(1)} %bitcast.14, ...), custom_call_target="tpu_custom_call", output_to_operand_aliasing={{0}: (2, {}), {1}: (3, {}), {2}: (4, {}), {3}: (5, {}), {4}... | custom-call | flops 134217728 | bytes 4194304 | tf_op jit(solution)/shard_map/attend/pallas_call | solution.py:275
  61.7 0.1 collective-permute-done.17.refs_0_
  61.9 1.6 %attend.11 = (bf16[128,32,128]{2,1,0:T(8,128)(2,1)}, f32[8,128]{1,0:T(8,128)S(1)}, f32[2,4,512,128]{3,2,1,0:T(8,128)S(1)}, f32[2,4,512,128]{3,2,1,0:T(8,128)S(1)...) custom-call(bf16[2,4,512,128]{3,2,1,0:T(8,128)(2,1)S(1)} %bitcast.15, ...), custom_call_target="tpu_custom_call", output_to_operand_aliasing={{1}: (2, {}), {2}: (3, {}), {3}: (4, {}), {4}: (5, {}), {5}... | custom-call | flops 134217728 | bytes 4194304 | tf_op jit(solution)/shard_map/attend/pallas_call | solution.py:275
  (11 shorter events, 0.3 us)
Async XLA Ops:
  2.1 6.1 %copy-start = (bf16[1040,128]{1,0:T(8,128)(2,1)S(1)}, bf16[1040,128]{1,0:T(8,128)(2,1)}, u32[]{:S(2)}) copy-start(bf16[1040,128]{1,0:T(8,128)(2,1)} %pack.1.own_ref) | copy-start | bytes 798724
  2.1 9.5 %collective-permute-start = (bf16[1040,128]{1,0:T(8,128)(2,1)}, bf16[1040,128]{1,0:T(8,128)(2,1)S(1)}, u32[]{:S(2)}, u32[]{:S(2)}) collective-permute-start(bf16[1040,128]{1,0:T(8,128)(2,1)} %pack.1.own_ref), channel_id=1, source_target_pairs={{0,8},{1,9},{2,10},{3,11},{4,12},{5,13},{6,14},{7,15},{8,24},{9,25... | collective-permute-start | bytes 798728 | tf_op jit(solution)/shard_map/ppermute | solution.py:333
  4.3 7.4 %collective-permute-start.6 = (bf16[1040,128]{1,0:T(8,128)(2,1)}, bf16[1040,128]{1,0:T(8,128)(2,1)S(1)}, u32[]{:S(2)}, u32[]{:S(2)}) collective-permute-start(bf16[1040,128]{1,0:T(8,128)(2,1)} %pack.1.own_ref), channel_id=1, source_target_pairs={{0,1},{1,0},{2,3},{3,2},{4,6},{5,7},{6,4},{7,5},{8,9},{9,8},{10,11... | collective-permute-start | bytes 798728 | tf_op jit(solution)/shard_map/ppermute | solution.py:333
  5.5 8.4 %collective-permute-start.7 = (bf16[1040,128]{1,0:T(8,128)(2,1)}, bf16[1040,128]{1,0:T(8,128)(2,1)S(1)}, u32[]{:S(2)}, u32[]{:S(2)}) collective-permute-start(bf16[1040,128]{1,0:T(8,128)(2,1)} %pack.1.own_ref), channel_id=1, source_target_pairs={{0,2},{1,3},{2,0},{3,1},{4,5},{5,4},{6,7},{7,6},{8,10},{9,11},{10,... | collective-permute-start | bytes 798728 | tf_op jit(solution)/shard_map/ppermute | solution.py:333
  14.0 5.8 %collective-permute-start.11 = (bf16[1040,128]{1,0:T(8,128)(2,1)S(1)}, bf16[1040,128]{1,0:T(8,128)(2,1)S(1)}, u32[]{:S(2)}, u32[]{:S(2)}) collective-permute-start(bf16[1040,128]{1,0:T(8,128)(2,1)S(1)} %collective-permute-done), channel_id=1, source_target_pairs={{0,1},{1,0},{2,3},{3,2},{4,6},{5,7},{6,4},{7,5},{8,9},{9,8},{10,11... | collective-permute-start | bytes 798728 | tf_op jit(solution)/shard_map/ppermute | solution.py:333
  14.0 8.1 %collective-permute-start.8 = (bf16[1040,128]{1,0:T(8,128)(2,1)S(1)}, bf16[1040,128]{1,0:T(8,128)(2,1)S(1)}, u32[]{:S(2)}, u32[]{:S(2)}) collective-permute-start(bf16[1040,128]{1,0:T(8,128)(2,1)S(1)} %collective-permute-done.6), channel_id=1, source_target_pairs={{0,2},{1,3},{2,0},{3,1},{4,5},{5,4},{6,7},{7,6},{8,10},{9,11},{10,... | collective-permute-start | bytes 798728 | tf_op jit(solution)/shard_map/ppermute | solution.py:333
  15.2 9.2 %collective-permute-start.1 = (bf16[1040,128]{1,0:T(8,128)(2,1)S(1)}, bf16[1040,128]{1,0:T(8,128)(2,1)S(1)}, u32[]{:S(2)}, u32[]{:S(2)}) collective-permute-start(bf16[1040,128]{1,0:T(8,128)(2,1)S(1)} %collective-permute-done), channel_id=1, source_target_pairs={{0,8},{1,9},{2,10},{3,11},{4,12},{5,13},{6,14},{7,15},{8,24},{9,25... | collective-permute-start | bytes 798728 | tf_op jit(solution)/shard_map/ppermute | solution.py:333
  19.8 10.1 %collective-permute-start.12 = (bf16[2080,128]{1,0:T(8,128)(2,1)S(1)}, bf16[2080,128]{1,0:T(8,128)(2,1)S(1)}, u32[]{:S(2)}, u32[]{:S(2)}) collective-permute-start(bf16[2080,128]{1,0:T(8,128)(2,1)S(1)} %pad_maximum_fusion.2), channel_id=1, source_target_pairs={{0,2},{1,3},{2,0},{3,1},{4,5},{5,4},{6,7},{7,6},{8,10},{9,11},{10,... | collective-permute-start | bytes 1597448 | tf_op jit(solution)/shard_map/ppermute | solution.py:333
  22.1 15.4 %collective-permute-start.9 = (bf16[4160,128]{1,0:T(8,128)(2,1)S(1)}, bf16[4160,128]{1,0:T(8,128)(2,1)S(1)}, u32[]{:S(2)}, u32[]{:S(2)}) collective-permute-start(bf16[4160,128]{1,0:T(8,128)(2,1)S(1)} %pad_maximum_fusion.refs_0_), channel_id=1, source_target_pairs={{0,4},{1,5},{2,6},{3,7},{4,0},{5,1},{6,2},{7,3},{8,12},{9,13},{10,... | collective-permute-start | bytes 3194888 | tf_op jit(solution)/shard_map/ppermute | solution.py:333
  24.4 13.7 %collective-permute-start.5 = (bf16[1040,128]{1,0:T(8,128)(2,1)S(1)}, bf16[1040,128]{1,0:T(8,128)(2,1)S(1)}, u32[]{:S(2)}, u32[]{:S(2)}) collective-permute-start(bf16[1040,128]{1,0:T(8,128)(2,1)S(1)} %collective-permute-done.1), channel_id=1, source_target_pairs={{0,1},{1,0},{2,3},{3,2},{4,6},{5,7},{6,4},{7,5},{8,9},{9,8},{10,11... | collective-permute-start | bytes 798728 | tf_op jit(solution)/shard_map/ppermute | solution.py:333
  24.9 10.3 %collective-permute-start.2 = (bf16[1040,128]{1,0:T(8,128)(2,1)S(1)}, bf16[1040,128]{1,0:T(8,128)(2,1)S(1)}, u32[]{:S(2)}, u32[]{:S(2)}) collective-permute-start(bf16[1040,128]{1,0:T(8,128)(2,1)S(1)} %collective-permute-done.1), channel_id=1, source_target_pairs={{0,8},{1,9},{2,10},{3,11},{4,12},{5,13},{6,14},{7,15},{8,24},{9,25... | collective-permute-start | bytes 798728 | tf_op jit(solution)/shard_map/ppermute | solution.py:333
  30.0 9.7 %collective-permute-start.13 = (bf16[4160,128]{1,0:T(8,128)(2,1)S(1)}, bf16[4160,128]{1,0:T(8,128)(2,1)S(1)}, u32[]{:S(2)}, u32[]{:S(2)}) collective-permute-start(bf16[4160,128]{1,0:T(8,128)(2,1)S(1)} %constant_dynamic-update-slice_fusion.refs_0_), channel_id=1, source_target_pairs={{0,4},{1,5},{2,6},{3,7},{4,0},{5,1},{6,2},{7,3},{8,12},{9,13},{10,... | collective-permute-start | bytes 3194888 | tf_op jit(solution)/shard_map/ppermute | solution.py:333
  35.2 15.4 %collective-permute-start.3 = (bf16[1040,128]{1,0:T(8,128)(2,1)S(1)}, bf16[1040,128]{1,0:T(8,128)(2,1)S(1)}, u32[]{:S(2)}, u32[]{:S(2)}) collective-permute-start(bf16[1040,128]{1,0:T(8,128)(2,1)S(1)} %collective-permute-done.2), channel_id=1, source_target_pairs={{0,1},{1,0},{2,3},{3,2},{4,6},{5,7},{6,4},{7,5},{8,9},{9,8},{10,11... | collective-permute-start | bytes 798728 | tf_op jit(solution)/shard_map/ppermute | solution.py:333
  36.3 14.3 %collective-permute-start.15 = (bf16[1040,128]{1,0:T(8,128)(2,1)S(1)}, bf16[1040,128]{1,0:T(8,128)(2,1)S(1)}, u32[]{:S(2)}, u32[]{:S(2)}) collective-permute-start(bf16[1040,128]{1,0:T(8,128)(2,1)S(1)} %collective-permute-done.2), channel_id=1, source_target_pairs={{0,2},{1,3},{2,0},{3,1},{4,5},{5,4},{6,7},{7,6},{8,10},{9,11},{10,... | collective-permute-start | bytes 798728 | tf_op jit(solution)/shard_map/ppermute | solution.py:333
  38.1 11.7 %collective-permute-start.10 = (bf16[2080,128]{1,0:T(8,128)(2,1)S(1)}, bf16[2080,128]{1,0:T(8,128)(2,1)S(1)}, u32[]{:S(2)}, u32[]{:S(2)}) collective-permute-start(bf16[2080,128]{1,0:T(8,128)(2,1)S(1)} %pad_maximum_fusion.1), channel_id=1, source_target_pairs={{0,2},{1,3},{2,0},{3,1},{4,5},{5,4},{6,7},{7,6},{8,10},{9,11},{10,... | collective-permute-start | bytes 1597448 | tf_op jit(solution)/shard_map/ppermute | solution.py:333
  49.9 4.1 %collective-permute-start.14 = (bf16[4160,128]{1,0:T(8,128)(2,1)S(1)}, bf16[4160,128]{1,0:T(8,128)(2,1)S(1)}, u32[]{:S(2)}, u32[]{:S(2)}) collective-permute-start(bf16[4160,128]{1,0:T(8,128)(2,1)S(1)} %constant_dynamic-update-slice_fusion.3.refs_0_), channel_id=1, source_target_pairs={{0,4},{1,5},{2,6},{3,7},{4,0},{5,1},{6,2},{7,3},{8,12},{9,13},{10,... | collective-permute-start | bytes 3194888 | tf_op jit(solution)/shard_map/ppermute | solution.py:333
  50.7 3.4 %collective-permute-start.16 = (bf16[3120,128]{1,0:T(8,128)(2,1)S(1)}, bf16[3120,128]{1,0:T(8,128)(2,1)S(1)}, u32[]{:S(2)}, u32[]{:S(2)}) collective-permute-start(bf16[3120,128]{1,0:T(8,128)(2,1)S(1)} %constant_dynamic-update-slice_fusion.6.refs_1_), channel_id=1, source_target_pairs={{0,4},{1,5},{2,6},{3,7},{4,0},{5,1},{6,2},{7,3},{8,12},{9,13},{10,... | collective-permute-start | bytes 2396168 | tf_op jit(solution)/shard_map/ppermute | solution.py:333
  50.7 5.6 %collective-permute-start.4 = (bf16[1040,128]{1,0:T(8,128)(2,1)S(1)}, bf16[1040,128]{1,0:T(8,128)(2,1)S(1)}, u32[]{:S(2)}, u32[]{:S(2)}) collective-permute-start(bf16[1040,128]{1,0:T(8,128)(2,1)S(1)} %collective-permute-done.3), channel_id=1, source_target_pairs={{0,2},{1,3},{2,0},{3,1},{4,5},{5,4},{6,7},{7,6},{8,10},{9,11},{10,... | collective-permute-start | bytes 798728 | tf_op jit(solution)/shard_map/ppermute | solution.py:333
  56.4 5.5 %collective-permute-start.17 = (bf16[1040,128]{1,0:T(8,128)(2,1)S(1)}, bf16[1040,128]{1,0:T(8,128)(2,1)S(1)}, u32[]{:S(2)}, u32[]{:S(2)}) collective-permute-start(bf16[1040,128]{1,0:T(8,128)(2,1)S(1)} %collective-permute-done.4.refs_0_), channel_id=1, source_target_pairs={{0,4},{1,5},{2,6},{3,7},{4,0},{5,1},{6,2},{7,3},{8,12},{9,13},{10,... | collective-permute-start | bytes 798728 | tf_op jit(solution)/shard_map/ppermute | solution.py:333
